TPU v7x, 512 devices: a whole 4x4x16 slice. The times are simulated.
512 devices in a mesh: queue: 64 (over x_lo, z, core), space: 8 (over y, x_hi).
Axes of the slice: x: 4 (x_hi: 2, x_lo: 2; x = x_hi * 2 + x_lo), y: 4, z: 16, core: 2. Of those that a mesh axis runs over, the one named last changes fastest.
Arguments:
- hidden: bfloat16 [64, 192, 3072], P('queue', 'space')
- qkv_weight: bfloat16 [3, 3072, 2048], P(None, 'queue', 'space'), may hold values from -0.109375 to 0.109375
- out_weight: bfloat16 [3072, 2048], P('queue', 'space'), may hold values from -0.125 to 0.125
- mod_weight: bfloat16 [256, 3, 3072], P(None, None, 'space'), may hold values from -0.375 to 0.375
- slot_frame: int32 [64], replicated, may hold values from 0 to 63, as said below
- levels: int32 [64], replicated, may hold values from 2 to 11, as said below
- timesteps: int32 [12], replicated, may hold values from 40 to 996, as said below
Outputs:
- velocity: bfloat16 [2, 64, 192, 3072], P(None, 'queue', 'space')
- latents: bfloat16 [64, 192, 3072], P('queue', 'space')
Inputs may be any that keep to these rules, and one draw needn't show every extreme that they name: `slot_frame`: slot q holds frame (q - r) mod 64 for one r of the draw. `levels`: never falling from frame to frame; frame 0 has level 2 and the last frame level 11. `timesteps`: strictly rising.
All inputs are finite; a program needn't handle non-finite values.
Results may differ from a plain program's by a relative error of at most 0.023.
Values may be sent and summed in bfloat16 or wider, within the bound.
A program may use at most 64 MiB of HBM per device.

v0:
```python
import math

import jax
import jax.numpy as jnp
from jax import lax
from jax.sharding import PartitionSpec as P

HEAD_DIM = 128
FREQ = 256
WINDOW = 16
STEPS = 2


def from_behind(block, axis, distance):
    devices = range(lax.axis_size(axis))
    route = [((i - distance) % len(devices), i) for i in devices]
    return lax.ppermute(block, axis, route)


def embed_time(t_now):
    half_freq = FREQ // 2
    omega = jnp.exp(-math.log(10000.0) * jnp.arange(half_freq).astype(jnp.float32) / half_freq)
    angles = t_now * omega
    return jnp.concatenate([jnp.cos(angles), jnp.sin(angles)], axis=-1).astype(jnp.bfloat16)


def rms_heads(values):
    wide = values.astype(jnp.float32)
    return (wide / jnp.sqrt(jnp.mean(wide * wide, axis=-1, keepdims=True) + 1e-06)).astype(
        jnp.bfloat16
    )


def attend_window(query_hat, window_kv, valid_mask):
    scores = jnp.einsum(
        "phc,wphc->wph", query_hat, window_kv[:, 0], preferred_element_type=jnp.float32
    )
    expo = jnp.exp(scores * (1.0 / math.sqrt(HEAD_DIM))) * valid_mask[:, None, None]
    denominator = jnp.sum(expo, axis=0, keepdims=True)
    attn_weights = (expo / denominator).astype(jnp.bfloat16)
    attended = jnp.einsum(
        "wph,wphc->phc", attn_weights, window_kv[:, 1], preferred_element_type=jnp.float32
    )
    return attended.astype(jnp.bfloat16)


def shards(hidden, qkv_weight, out_weight, mod_weight, slot_frame, levels, timesteps):
    slot_count = lax.axis_size("queue")
    own_frame = slot_frame[lax.axis_index("queue")]
    half_window = WINDOW // 2
    w_qkv, w_out = (
        lax.all_gather(qkv_weight, "queue", axis=1, tiled=True),
        lax.all_gather(out_weight, "queue", axis=0, tiled=True),
    )
    width_dev = w_out.shape[1]
    heads_dev = width_dev // HEAD_DIM
    offsets = jnp.arange(-half_window, half_window)
    target = own_frame + offsets
    window_mask = ((target >= 0) & (target < slot_count)).astype(jnp.float32)
    state = hidden[0]
    outputs = []
    for step_index in range(STEPS):
        level_now = levels[own_frame] - step_index
        t_now = timesteps[level_now].astype(jnp.float32)
        t_next = timesteps[level_now - 1].astype(jnp.float32)
        sigma_step = (t_next - t_now) / 1000.0
        embedding = embed_time(t_now)
        mod_part = jnp.einsum(
            "f,fkd->kd", embedding, mod_weight, preferred_element_type=jnp.float32
        )
        mod_full = lax.all_gather(mod_part, "space", axis=1, tiled=True)
        mod_shift = mod_full[0]
        mod_scale = mod_full[1]
        mod_gate = mod_full[2]
        current = state.astype(jnp.float32)
        row_mean = jnp.mean(current, axis=-1, keepdims=True)
        centered = current - row_mean
        row_var = jnp.mean(centered * centered, axis=-1, keepdims=True)
        normed = (centered / jnp.sqrt(row_var + 1e-06) * (1.0 + mod_scale) + mod_shift).astype(
            jnp.bfloat16
        )
        projected = jnp.einsum(
            "rd,kdc->rkc",
            lax.all_gather(normed, "space", axis=0, tiled=True),
            w_qkv,
            preferred_element_type=jnp.float32,
        ).astype(jnp.bfloat16)
        frame_rows = projected.shape[0]
        query_hat = rms_heads(projected[:, 0].reshape(frame_rows, heads_dev, HEAD_DIM))
        key_hat = rms_heads(projected[:, 1].reshape(frame_rows, heads_dev, HEAD_DIM))
        values = projected[:, 2].reshape(frame_rows, heads_dev, HEAD_DIM)
        own_kv = jnp.stack([key_hat, values])
        key_list = []
        for offset in range(-half_window, half_window):
            if offset == 0:
                key_list.append(own_kv)
            else:
                key_list.append(from_behind(own_kv, "queue", -offset))
        attended = attend_window(query_hat, jnp.stack(key_list), window_mask)
        attended = attended.reshape(frame_rows, width_dev)
        branch = lax.psum_scatter(
            jnp.einsum("rc,dc->rd", attended, w_out, preferred_element_type=jnp.float32).astype(
                jnp.bfloat16
            ),
            "space",
            scatter_dimension=0,
            tiled=True,
        ).astype(jnp.float32)
        velocity_now = current + mod_gate * branch
        outputs.append(velocity_now.astype(jnp.bfloat16))
        state = (current + sigma_step * velocity_now).astype(jnp.bfloat16)
    return (jnp.stack(outputs)[:, None], state[None])


def solution(mesh):
    in_specs = (
        P("queue", "space", None),
        P(None, "queue", "space"),
        P("queue", "space"),
        P(None, None, "space"),
        P(),
        P(),
        P(),
    )
    out_specs = (P(None, "queue", "space", None), P("queue", "space", None))
    return jax.shard_map(shards, mesh=mesh, in_specs=in_specs, out_specs=out_specs, check_vma=False)
```

profile of v0, /device:TPU:1, one launch (start us, length us, event | category | flops | bytes accessed | tf_op | source)
XLA Modules:
  0.0 800.1 jit_solution(2288289960556093177)
XLA Ops:
  16.2 1.4 fusion.69
  18.6 29.2 %all_gather.18 = f32[3,3072]{1,0:T(4,128)S(1)} all-gather(f32[3,384]{1,0:T(4,128)S(1)} %bitcast.221), channel_id=1, replica_groups=mesh['queue'=64,'space'=8] {'space'}, dimensions={1}, use_global_device_ids=true | all-gather | bytes 41472 | tf_op jit(solution)/shard_map/all_gather | solution.py:71
  50.0 1.7 fusion.32
  54.0 69.4 %all-gather.5.cloned.1.call-done = bf16[192,3072]{1,0:T(8,128)(2,1)} async-done(((bf16[24,3072]{1,0:T(8,128)(2,1)}), bf16[192,3072]{1,0:T(8,128)(2,1)}) %all-gather.5.cloned.1.call-update) | async-done | bytes 1179664 | tf_op jit(solution)/shard_map/all_gather | solution.py:84
  123.4 128.5 %all-gather.7.cloned.1.call-done = bf16[3,3072,256]{2,1,0:T(8,128)(2,1)} async-done(((bf16[3,48,256]{2,1,0:T(8,128)(2,1)}), bf16[3,3072,256]{2,1,0:T(8,128)(2,1)}) %all-gather.7.cloned.1.call-update) | async-done | bytes 4718608 | tf_op jit(solution)/shard_map/all_gather | solution.py:52
  251.8 3.8 convolution_convert_fusion.3
  256.8 5.2 collective-permute-start
  262.1 4.8 collective-permute-start.1
  266.9 3.8 collective-permute-start.2
  270.7 4.2 collective-permute-start.3
  274.9 2.0 collective-permute-start.4
  277.6 5.5 collective-permute-start.5
  283.3 16.4 %collective-permute-done.1 = bf16[2,192,2,128]{3,2,1,0:T(2,128)(2,1)S(1)} collective-permute-done((bf16[2,192,2,128]{3,2,1,0:T(2,128)(2,1)S(1)}, bf16[2,192,2,128]{3,2,1,0:T(2,128)(2,1)S(1)}, u32[]{:S(2)}, u32[]{:S(2)}) %collective-permute-start.1) | collective-permute-done | bytes 196640 | tf_op jit(solution)/shard_map/ppermute | solution.py:17
  299.7 1.9 collective-permute-start.6
  301.8 9.2 %collective-permute-done.2 = bf16[2,192,2,128]{3,2,1,0:T(2,128)(2,1)S(1)} collective-permute-done((bf16[2,192,2,128]{3,2,1,0:T(2,128)(2,1)S(1)}, bf16[2,192,2,128]{3,2,1,0:T(2,128)(2,1)S(1)}, u32[]{:S(2)}, u32[]{:S(2)}) %collective-permute-start.2) | collective-permute-done | bytes 196640 | tf_op jit(solution)/shard_map/ppermute | solution.py:17
  311.0 1.9 collective-permute-start.7
  313.1 12.1 %collective-permute-done.3 = bf16[2,192,2,128]{3,2,1,0:T(2,128)(2,1)S(1)} collective-permute-done((bf16[2,192,2,128]{3,2,1,0:T(2,128)(2,1)S(1)}, bf16[2,192,2,128]{3,2,1,0:T(2,128)(2,1)S(1)}, u32[]{:S(2)}, u32[]{:S(2)}) %collective-permute-start.3) | collective-permute-done | bytes 196640 | tf_op jit(solution)/shard_map/ppermute | solution.py:17
  325.2 4.4 collective-permute-start.8
  329.7 1.4 collective-permute-done.4
  331.1 5.6 collective-permute-start.9
  336.9 6.1 collective-permute-start.10
  343.1 4.4 collective-permute-start.11
  347.7 3.4 collective-permute-start.12
  351.4 4.1 collective-permute-start.13
  355.7 3.8 collective-permute-start.14
  359.9 3.4 collective-permute-done.11
  363.4 6.4 collective-permute-done.12
  370.0 9.2 %collective-permute-done.13 = bf16[2,192,2,128]{3,2,1,0:T(2,128)(2,1)S(1)} collective-permute-done((bf16[2,192,2,128]{3,2,1,0:T(2,128)(2,1)S(1)}, bf16[2,192,2,128]{3,2,1,0:T(2,128)(2,1)S(1)}, u32[]{:S(2)}, u32[]{:S(2)}) %collective-permute-start.13) | collective-permute-done | bytes 196640 | tf_op jit(solution)/shard_map/ppermute | solution.py:17
  379.4 22.7 %collective-permute-done.14 = bf16[2,192,2,128]{3,2,1,0:T(2,128)(2,1)S(1)} collective-permute-done((bf16[2,192,2,128]{3,2,1,0:T(2,128)(2,1)S(1)}, bf16[2,192,2,128]{3,2,1,0:T(2,128)(2,1)S(1)}, u32[]{:S(2)}, u32[]{:S(2)}) %collective-permute-start.14) | collective-permute-done | bytes 196640 | tf_op jit(solution)/shard_map/ppermute | solution.py:17
  402.2 3.8 slice_bitcast_fusion.2
  408.7 3.1 convolution_convert_fusion.1
  412.8 28.4 %all_gather.22 = f32[3,3072]{1,0:T(4,128)S(1)} all-gather(f32[3,384]{1,0:T(4,128)S(1)} %bitcast.220), channel_id=1, replica_groups=mesh['queue'=64,'space'=8] {'space'}, dimensions={1}, use_global_device_ids=true | all-gather | bytes 41472 | tf_op jit(solution)/shard_map/all_gather | solution.py:71
  441.2 51.6 %reduce-scatter.3.cloned.1.call-done = bf16[24,3072]{1,0:T(8,128)(2,1)} async-done(((bf16[192,3072]{1,0:T(8,128)(2,1)}), bf16[24,3072]{1,0:T(8,128)(2,1)}) %reduce-scatter.3.cloned.1.call-update) | async-done | bytes 147472 | tf_op jit(solution)/shard_map/reduce_scatter | solution.py:101
  495.1 63.5 %all-gather.11.cloned.1.call-done = bf16[192,3072]{1,0:T(8,128)(2,1)} async-done(((bf16[24,3072]{1,0:T(8,128)(2,1)}), bf16[192,3072]{1,0:T(8,128)(2,1)}) %all-gather.11.cloned.1.call-update) | async-done | bytes 1179664 | tf_op jit(solution)/shard_map/all_gather | solution.py:84
  558.6 3.8 convolution_convert_fusion.2
  563.6 7.4 collective-permute-start.15
  571.0 9.5 %collective-permute-start.16 = (bf16[2,192,2,128]{3,2,1,0:T(2,128)(2,1)S(1)}, bf16[2,192,2,128]{3,2,1,0:T(2,128)(2,1)S(1)}, u32[]{:S(2)}, u32[]{:S(2)}) collective-permute-start(bf16[2,192,2,128]{3,2,1,0:T(2,128)(2,1)S(1)} %pad_maximum_fusion.1), channel_id=1, source_target_pairs={{456,0},{464,8},{472,16},{480,24},{488,32},{496,40},{504,48},{0,56... | collective-permute-start | bytes 589832 | tf_op jit(solution)/shard_map/ppermute | solution.py:17
  580.5 2.5 collective-permute-start.17
  583.0 2.1 collective-permute-start.18
  585.1 2.4 collective-permute-start.19
  588.2 11.5 %collective-permute-start.20 = (bf16[2,192,2,128]{3,2,1,0:T(2,128)(2,1)S(1)}, bf16[2,192,2,128]{3,2,1,0:T(2,128)(2,1)S(1)}, u32[]{:S(2)}, u32[]{:S(2)}) collective-permute-start(bf16[2,192,2,128]{3,2,1,0:T(2,128)(2,1)S(1)} %pad_maximum_fusion.1), channel_id=1, source_target_pairs={{488,0},{496,8},{504,16},{0,24},{8,32},{16,40},{24,48},{32,56},{40... | collective-permute-start | bytes 589832 | tf_op jit(solution)/shard_map/ppermute | solution.py:17
  599.9 10.3 %collective-permute-done.16 = bf16[2,192,2,128]{3,2,1,0:T(2,128)(2,1)S(1)} collective-permute-done((bf16[2,192,2,128]{3,2,1,0:T(2,128)(2,1)S(1)}, bf16[2,192,2,128]{3,2,1,0:T(2,128)(2,1)S(1)}, u32[]{:S(2)}, u32[]{:S(2)}) %collective-permute-start.16) | collective-permute-done | bytes 196640 | tf_op jit(solution)/shard_map/ppermute | solution.py:17
  610.2 1.9 collective-permute-start.21
  612.3 6.7 collective-permute-done.17
  619.0 1.9 collective-permute-start.22
  621.1 5.7 collective-permute-done.18
  626.7 3.8 collective-permute-start.23
  630.7 4.1 collective-permute-done.19
  634.8 3.8 collective-permute-start.24
  638.8 3.7 collective-permute-done.20
  642.5 2.4 collective-permute-start.25
  645.0 1.6 collective-permute-done.21
  646.7 2.4 collective-permute-start.26
  649.2 6.3 collective-permute-start.27
  655.9 5.9 collective-permute-start.28
  661.9 4.0 collective-permute-start.29
  666.4 6.8 collective-permute-done.27
  673.4 10.6 %collective-permute-done.28 = bf16[2,192,2,128]{3,2,1,0:T(2,128)(2,1)S(1)} collective-permute-done((bf16[2,192,2,128]{3,2,1,0:T(2,128)(2,1)S(1)}, bf16[2,192,2,128]{3,2,1,0:T(2,128)(2,1)S(1)}, u32[]{:S(2)}, u32[]{:S(2)}) %collective-permute-start.28) | collective-permute-done | bytes 196640 | tf_op jit(solution)/shard_map/ppermute | solution.py:17
  684.2 14.9 %collective-permute-done.29 = bf16[2,192,2,128]{3,2,1,0:T(2,128)(2,1)S(1)} collective-permute-done((bf16[2,192,2,128]{3,2,1,0:T(2,128)(2,1)S(1)}, bf16[2,192,2,128]{3,2,1,0:T(2,128)(2,1)S(1)}, u32[]{:S(2)}, u32[]{:S(2)}) %collective-permute-start.29) | collective-permute-done | bytes 196640 | tf_op jit(solution)/shard_map/ppermute | solution.py:17
  699.3 3.5 slice_bitcast_fusion
  704.2 2.5 fusion.2
  706.8 1.7 convolution_convert_fusion
  709.2 81.7 %reduce-scatter.5.cloned.1.call-done = bf16[24,3072]{1,0:T(8,128)(2,1)} async-done(((bf16[192,3072]{1,0:T(8,128)(2,1)}), bf16[24,3072]{1,0:T(8,128)(2,1)}) %reduce-scatter.5.cloned.1.call-update) | async-done | bytes 147472 | tf_op jit(solution)/shard_map/reduce_scatter | solution.py:101
  790.9 1.6 fusion.41
  (126 shorter events, 23.5 us)
Async XLA Ops:
  7.2 11.3 %copy-start = (bf16[256,3,384]{2,0,1:T(8,128)(2,1)S(1)}, bf16[256,3,384]{2,0,1:T(8,128)(2,1)}, u32[]{:S(2)}) copy-start(bf16[256,3,384]{2,0,1:T(8,128)(2,1)} %param.10) | copy-start | bytes 1769476
  7.2 116.2 %all-gather.5.cloned.1.call-start = ((), (), s32[]{:S(2)}) async-start(), calls=%async_computation.2 | async-start | bytes 1327104 | tf_op jit(solution)/shard_map/all_gather | solution.py:84
  51.8 200.1 %all-gather.7.cloned.1.call-start = ((), (), s32[]{:S(2)}) async-start(), calls=%async_computation.3 | async-start | bytes 4792320 | tf_op jit(solution)/shard_map/all_gather | solution.py:52
  52.5 356.2 %all-gather.9.cloned.1.call-start = ((), (), s32[]{:S(2)}) async-start(), calls=%async_computation.4 | async-start | bytes 1597440 | tf_op jit(solution)/shard_map/all_gather | solution.py:53
  53.2 439.6 %reduce-scatter.3.cloned.1.call-start = ((), (), s32[]{:S(2)}) async-start(), calls=%async_computation.5 | async-start | bytes 1327104 | tf_op jit(solution)/shard_map/reduce_scatter | solution.py:101
  256.8 20.8 %collective-permute-start = (bf16[2,192,2,128]{3,2,1,0:T(2,128)(2,1)S(1)}, bf16[2,192,2,128]{3,2,1,0:T(2,128)(2,1)S(1)}, u32[]{:S(2)}, u32[]{:S(2)}) collective-permute-start(bf16[2,192,2,128]{3,2,1,0:T(2,128)(2,1)S(1)} %pad_maximum_fusion), channel_id=1, source_target_pairs={{448,0},{456,8},{464,16},{472,24},{480,32},{488,40},{496,48},{504,... | collective-permute-start | bytes 589832 | tf_op jit(solution)/shard_map/ppermute | solution.py:17
  262.1 37.6 %collective-permute-start.1 = (bf16[2,192,2,128]{3,2,1,0:T(2,128)(2,1)S(1)}, bf16[2,192,2,128]{3,2,1,0:T(2,128)(2,1)S(1)}, u32[]{:S(2)}, u32[]{:S(2)}) collective-permute-start(bf16[2,192,2,128]{3,2,1,0:T(2,128)(2,1)S(1)} %pad_maximum_fusion), channel_id=1, source_target_pairs={{456,0},{464,8},{472,16},{480,24},{488,32},{496,40},{504,48},{0,56... | collective-permute-start | bytes 589832 | tf_op jit(solution)/shard_map/ppermute | solution.py:17
  266.9 44.1 %collective-permute-start.2 = (bf16[2,192,2,128]{3,2,1,0:T(2,128)(2,1)S(1)}, bf16[2,192,2,128]{3,2,1,0:T(2,128)(2,1)S(1)}, u32[]{:S(2)}, u32[]{:S(2)}) collective-permute-start(bf16[2,192,2,128]{3,2,1,0:T(2,128)(2,1)S(1)} %pad_maximum_fusion), channel_id=1, source_target_pairs={{464,0},{472,8},{480,16},{488,24},{496,32},{504,40},{0,48},{8,56},... | collective-permute-start | bytes 589832 | tf_op jit(solution)/shard_map/ppermute | solution.py:17
  270.7 54.5 %collective-permute-start.3 = (bf16[2,192,2,128]{3,2,1,0:T(2,128)(2,1)S(1)}, bf16[2,192,2,128]{3,2,1,0:T(2,128)(2,1)S(1)}, u32[]{:S(2)}, u32[]{:S(2)}) collective-permute-start(bf16[2,192,2,128]{3,2,1,0:T(2,128)(2,1)S(1)} %pad_maximum_fusion), channel_id=1, source_target_pairs={{472,0},{480,8},{488,16},{496,24},{504,32},{0,40},{8,48},{16,56},{... | collective-permute-start | bytes 589832 | tf_op jit(solution)/shard_map/ppermute | solution.py:17
  274.9 56.2 %collective-permute-start.4 = (bf16[2,192,2,128]{3,2,1,0:T(2,128)(2,1)S(1)}, bf16[2,192,2,128]{3,2,1,0:T(2,128)(2,1)S(1)}, u32[]{:S(2)}, u32[]{:S(2)}) collective-permute-start(bf16[2,192,2,128]{3,2,1,0:T(2,128)(2,1)S(1)} %pad_maximum_fusion), channel_id=1, source_target_pairs={{480,0},{488,8},{496,16},{504,24},{0,32},{8,40},{16,48},{24,56},{3... | collective-permute-start | bytes 589832 | tf_op jit(solution)/shard_map/ppermute | solution.py:17
  277.6 59.2 %collective-permute-start.5 = (bf16[2,192,2,128]{3,2,1,0:T(2,128)(2,1)S(1)}, bf16[2,192,2,128]{3,2,1,0:T(2,128)(2,1)S(1)}, u32[]{:S(2)}, u32[]{:S(2)}) collective-permute-start(bf16[2,192,2,128]{3,2,1,0:T(2,128)(2,1)S(1)} %pad_maximum_fusion), channel_id=1, source_target_pairs={{488,0},{496,8},{504,16},{0,24},{8,32},{16,40},{24,48},{32,56},{40... | collective-permute-start | bytes 589832 | tf_op jit(solution)/shard_map/ppermute | solution.py:17
  299.7 43.4 %collective-permute-start.6 = (bf16[2,192,2,128]{3,2,1,0:T(2,128)(2,1)S(1)}, bf16[2,192,2,128]{3,2,1,0:T(2,128)(2,1)S(1)}, u32[]{:S(2)}, u32[]{:S(2)}) collective-permute-start(bf16[2,192,2,128]{3,2,1,0:T(2,128)(2,1)S(1)} %pad_maximum_fusion), channel_id=1, source_target_pairs={{496,0},{504,8},{0,16},{8,24},{16,32},{24,40},{32,48},{40,56},{48,... | collective-permute-start | bytes 589832 | tf_op jit(solution)/shard_map/ppermute | solution.py:17
  311.0 36.6 %collective-permute-start.7 = (bf16[2,192,2,128]{3,2,1,0:T(2,128)(2,1)S(1)}, bf16[2,192,2,128]{3,2,1,0:T(2,128)(2,1)S(1)}, u32[]{:S(2)}, u32[]{:S(2)}) collective-permute-start(bf16[2,192,2,128]{3,2,1,0:T(2,128)(2,1)S(1)} %pad_maximum_fusion), channel_id=1, source_target_pairs={{504,0},{0,8},{8,16},{16,24},{24,32},{32,40},{40,48},{48,56},{56,6... | collective-permute-start | bytes 589832 | tf_op jit(solution)/shard_map/ppermute | solution.py:17
  325.2 26.2 %collective-permute-start.8 = (bf16[2,192,2,128]{3,2,1,0:T(2,128)(2,1)S(1)}, bf16[2,192,2,128]{3,2,1,0:T(2,128)(2,1)S(1)}, u32[]{:S(2)}, u32[]{:S(2)}) collective-permute-start(bf16[2,192,2,128]{3,2,1,0:T(2,128)(2,1)S(1)} %pad_maximum_fusion), channel_id=1, source_target_pairs={{8,0},{16,8},{24,16},{32,24},{40,32},{48,40},{56,48},{64,56},{72,6... | collective-permute-start | bytes 589832 | tf_op jit(solution)/shard_map/ppermute | solution.py:17
  331.1 24.6 %collective-permute-start.9 = (bf16[2,192,2,128]{3,2,1,0:T(2,128)(2,1)S(1)}, bf16[2,192,2,128]{3,2,1,0:T(2,128)(2,1)S(1)}, u32[]{:S(2)}, u32[]{:S(2)}) collective-permute-start(bf16[2,192,2,128]{3,2,1,0:T(2,128)(2,1)S(1)} %pad_maximum_fusion), channel_id=1, source_target_pairs={{16,0},{24,8},{32,16},{40,24},{48,32},{56,40},{64,48},{72,56},{80,... | collective-permute-start | bytes 589832 | tf_op jit(solution)/shard_map/ppermute | solution.py:17
  336.9 22.8 %collective-permute-start.10 = (bf16[2,192,2,128]{3,2,1,0:T(2,128)(2,1)S(1)}, bf16[2,192,2,128]{3,2,1,0:T(2,128)(2,1)S(1)}, u32[]{:S(2)}, u32[]{:S(2)}) collective-permute-start(bf16[2,192,2,128]{3,2,1,0:T(2,128)(2,1)S(1)} %pad_maximum_fusion), channel_id=1, source_target_pairs={{24,0},{32,8},{40,16},{48,24},{56,32},{64,40},{72,48},{80,56},{88,... | collective-permute-start | bytes 589832 | tf_op jit(solution)/shard_map/ppermute | solution.py:17
  343.1 20.1 %collective-permute-start.11 = (bf16[2,192,2,128]{3,2,1,0:T(2,128)(2,1)S(1)}, bf16[2,192,2,128]{3,2,1,0:T(2,128)(2,1)S(1)}, u32[]{:S(2)}, u32[]{:S(2)}) collective-permute-start(bf16[2,192,2,128]{3,2,1,0:T(2,128)(2,1)S(1)} %pad_maximum_fusion), channel_id=1, source_target_pairs={{32,0},{40,8},{48,16},{56,24},{64,32},{72,40},{80,48},{88,56},{96,... | collective-permute-start | bytes 589832 | tf_op jit(solution)/shard_map/ppermute | solution.py:17
  347.7 22.2 %collective-permute-start.12 = (bf16[2,192,2,128]{3,2,1,0:T(2,128)(2,1)S(1)}, bf16[2,192,2,128]{3,2,1,0:T(2,128)(2,1)S(1)}, u32[]{:S(2)}, u32[]{:S(2)}) collective-permute-start(bf16[2,192,2,128]{3,2,1,0:T(2,128)(2,1)S(1)} %pad_maximum_fusion), channel_id=1, source_target_pairs={{40,0},{48,8},{56,16},{64,24},{72,32},{80,40},{88,48},{96,56},{104... | collective-permute-start | bytes 589832 | tf_op jit(solution)/shard_map/ppermute | solution.py:17
  351.4 27.8 %collective-permute-start.13 = (bf16[2,192,2,128]{3,2,1,0:T(2,128)(2,1)S(1)}, bf16[2,192,2,128]{3,2,1,0:T(2,128)(2,1)S(1)}, u32[]{:S(2)}, u32[]{:S(2)}) collective-permute-start(bf16[2,192,2,128]{3,2,1,0:T(2,128)(2,1)S(1)} %pad_maximum_fusion), channel_id=1, source_target_pairs={{48,0},{56,8},{64,16},{72,24},{80,32},{88,40},{96,48},{104,56},{11... | collective-permute-start | bytes 589832 | tf_op jit(solution)/shard_map/ppermute | solution.py:17
  355.7 46.3 %collective-permute-start.14 = (bf16[2,192,2,128]{3,2,1,0:T(2,128)(2,1)S(1)}, bf16[2,192,2,128]{3,2,1,0:T(2,128)(2,1)S(1)}, u32[]{:S(2)}, u32[]{:S(2)}) collective-permute-start(bf16[2,192,2,128]{3,2,1,0:T(2,128)(2,1)S(1)} %pad_maximum_fusion), channel_id=1, source_target_pairs={{56,0},{64,8},{72,16},{80,24},{88,32},{96,40},{104,48},{112,56},{1... | collective-permute-start | bytes 589832 | tf_op jit(solution)/shard_map/ppermute | solution.py:17
  407.5 85.4 %copy-start.2 = (bf16[1,24,3072]{2,1,0:T(8,128)(2,1)S(1)}, bf16[1,24,3072]{2,1,0:T(8,128)(2,1)}, u32[]{:S(2)}) copy-start(bf16[1,24,3072]{2,1,0:T(8,128)(2,1)} %param.7) | copy-start | bytes 442372
  411.8 146.8 %all-gather.11.cloned.1.call-start = ((), (), s32[]{:S(2)}) async-start(), calls=%async_computation.6 | async-start | bytes 1327104 | tf_op jit(solution)/shard_map/all_gather | solution.py:84
  495.0 295.9 %reduce-scatter.5.cloned.1.call-start = ((), (), s32[]{:S(2)}) async-start(), calls=%async_computation.7 | async-start | bytes 1327104 | tf_op jit(solution)/shard_map/reduce_scatter | solution.py:101
  563.6 24.6 %collective-permute-start.15 = (bf16[2,192,2,128]{3,2,1,0:T(2,128)(2,1)S(1)}, bf16[2,192,2,128]{3,2,1,0:T(2,128)(2,1)S(1)}, u32[]{:S(2)}, u32[]{:S(2)}) collective-permute-start(bf16[2,192,2,128]{3,2,1,0:T(2,128)(2,1)S(1)} %pad_maximum_fusion.1), channel_id=1, source_target_pairs={{448,0},{456,8},{464,16},{472,24},{480,32},{488,40},{496,48},{504,... | collective-permute-start | bytes 589832 | tf_op jit(solution)/shard_map/ppermute | solution.py:17
  571.0 39.2 %collective-permute-start.16 = (bf16[2,192,2,128]{3,2,1,0:T(2,128)(2,1)S(1)}, bf16[2,192,2,128]{3,2,1,0:T(2,128)(2,1)S(1)}, u32[]{:S(2)}, u32[]{:S(2)}) collective-permute-start(bf16[2,192,2,128]{3,2,1,0:T(2,128)(2,1)S(1)} %pad_maximum_fusion.1), channel_id=1, source_target_pairs={{456,0},{464,8},{472,16},{480,24},{488,32},{496,40},{504,48},{0,56... | collective-permute-start | bytes 589832 | tf_op jit(solution)/shard_map/ppermute | solution.py:17
  580.5 38.5 %collective-permute-start.17 = (bf16[2,192,2,128]{3,2,1,0:T(2,128)(2,1)S(1)}, bf16[2,192,2,128]{3,2,1,0:T(2,128)(2,1)S(1)}, u32[]{:S(2)}, u32[]{:S(2)}) collective-permute-start(bf16[2,192,2,128]{3,2,1,0:T(2,128)(2,1)S(1)} %pad_maximum_fusion.1), channel_id=1, source_target_pairs={{464,0},{472,8},{480,16},{488,24},{496,32},{504,40},{0,48},{8,56},... | collective-permute-start | bytes 589832 | tf_op jit(solution)/shard_map/ppermute | solution.py:17
  583.0 43.7 %collective-permute-start.18 = (bf16[2,192,2,128]{3,2,1,0:T(2,128)(2,1)S(1)}, bf16[2,192,2,128]{3,2,1,0:T(2,128)(2,1)S(1)}, u32[]{:S(2)}, u32[]{:S(2)}) collective-permute-start(bf16[2,192,2,128]{3,2,1,0:T(2,128)(2,1)S(1)} %pad_maximum_fusion.1), channel_id=1, source_target_pairs={{472,0},{480,8},{488,16},{496,24},{504,32},{0,40},{8,48},{16,56},{... | collective-permute-start | bytes 589832 | tf_op jit(solution)/shard_map/ppermute | solution.py:17
  585.1 49.7 %collective-permute-start.19 = (bf16[2,192,2,128]{3,2,1,0:T(2,128)(2,1)S(1)}, bf16[2,192,2,128]{3,2,1,0:T(2,128)(2,1)S(1)}, u32[]{:S(2)}, u32[]{:S(2)}) collective-permute-start(bf16[2,192,2,128]{3,2,1,0:T(2,128)(2,1)S(1)} %pad_maximum_fusion.1), channel_id=1, source_target_pairs={{480,0},{488,8},{496,16},{504,24},{0,32},{8,40},{16,48},{24,56},{3... | collective-permute-start | bytes 589832 | tf_op jit(solution)/shard_map/ppermute | solution.py:17
  588.2 54.3 %collective-permute-start.20 = (bf16[2,192,2,128]{3,2,1,0:T(2,128)(2,1)S(1)}, bf16[2,192,2,128]{3,2,1,0:T(2,128)(2,1)S(1)}, u32[]{:S(2)}, u32[]{:S(2)}) collective-permute-start(bf16[2,192,2,128]{3,2,1,0:T(2,128)(2,1)S(1)} %pad_maximum_fusion.1), channel_id=1, source_target_pairs={{488,0},{496,8},{504,16},{0,24},{8,32},{16,40},{24,48},{32,56},{40... | collective-permute-start | bytes 589832 | tf_op jit(solution)/shard_map/ppermute | solution.py:17
  610.2 36.5 %collective-permute-start.21 = (bf16[2,192,2,128]{3,2,1,0:T(2,128)(2,1)S(1)}, bf16[2,192,2,128]{3,2,1,0:T(2,128)(2,1)S(1)}, u32[]{:S(2)}, u32[]{:S(2)}) collective-permute-start(bf16[2,192,2,128]{3,2,1,0:T(2,128)(2,1)S(1)} %pad_maximum_fusion.1), channel_id=1, source_target_pairs={{496,0},{504,8},{0,16},{8,24},{16,32},{24,40},{32,48},{40,56},{48,... | collective-permute-start | bytes 589832 | tf_op jit(solution)/shard_map/ppermute | solution.py:17
  619.0 30.2 %collective-permute-start.22 = (bf16[2,192,2,128]{3,2,1,0:T(2,128)(2,1)S(1)}, bf16[2,192,2,128]{3,2,1,0:T(2,128)(2,1)S(1)}, u32[]{:S(2)}, u32[]{:S(2)}) collective-permute-start(bf16[2,192,2,128]{3,2,1,0:T(2,128)(2,1)S(1)} %pad_maximum_fusion.1), channel_id=1, source_target_pairs={{504,0},{0,8},{8,16},{16,24},{24,32},{32,40},{40,48},{48,56},{56,6... | collective-permute-start | bytes 589832 | tf_op jit(solution)/shard_map/ppermute | solution.py:17
  626.7 29.1 %collective-permute-start.23 = (bf16[2,192,2,128]{3,2,1,0:T(2,128)(2,1)S(1)}, bf16[2,192,2,128]{3,2,1,0:T(2,128)(2,1)S(1)}, u32[]{:S(2)}, u32[]{:S(2)}) collective-permute-start(bf16[2,192,2,128]{3,2,1,0:T(2,128)(2,1)S(1)} %pad_maximum_fusion.1), channel_id=1, source_target_pairs={{8,0},{16,8},{24,16},{32,24},{40,32},{48,40},{56,48},{64,56},{72,6... | collective-permute-start | bytes 589832 | tf_op jit(solution)/shard_map/ppermute | solution.py:17
  634.8 27.1 %collective-permute-start.24 = (bf16[2,192,2,128]{3,2,1,0:T(2,128)(2,1)S(1)}, bf16[2,192,2,128]{3,2,1,0:T(2,128)(2,1)S(1)}, u32[]{:S(2)}, u32[]{:S(2)}) collective-permute-start(bf16[2,192,2,128]{3,2,1,0:T(2,128)(2,1)S(1)} %pad_maximum_fusion.1), channel_id=1, source_target_pairs={{16,0},{24,8},{32,16},{40,24},{48,32},{56,40},{64,48},{72,56},{80,... | collective-permute-start | bytes 589832 | tf_op jit(solution)/shard_map/ppermute | solution.py:17
  642.5 23.6 %collective-permute-start.25 = (bf16[2,192,2,128]{3,2,1,0:T(2,128)(2,1)S(1)}, bf16[2,192,2,128]{3,2,1,0:T(2,128)(2,1)S(1)}, u32[]{:S(2)}, u32[]{:S(2)}) collective-permute-start(bf16[2,192,2,128]{3,2,1,0:T(2,128)(2,1)S(1)} %pad_maximum_fusion.1), channel_id=1, source_target_pairs={{24,0},{32,8},{40,16},{48,24},{56,32},{64,40},{72,48},{80,56},{88,... | collective-permute-start | bytes 589832 | tf_op jit(solution)/shard_map/ppermute | solution.py:17
  646.7 19.6 %collective-permute-start.26 = (bf16[2,192,2,128]{3,2,1,0:T(2,128)(2,1)S(1)}, bf16[2,192,2,128]{3,2,1,0:T(2,128)(2,1)S(1)}, u32[]{:S(2)}, u32[]{:S(2)}) collective-permute-start(bf16[2,192,2,128]{3,2,1,0:T(2,128)(2,1)S(1)} %pad_maximum_fusion.1), channel_id=1, source_target_pairs={{32,0},{40,8},{48,16},{56,24},{64,32},{72,40},{80,48},{88,56},{96,... | collective-permute-start | bytes 589832 | tf_op jit(solution)/shard_map/ppermute | solution.py:17
  649.2 24.0 %collective-permute-start.27 = (bf16[2,192,2,128]{3,2,1,0:T(2,128)(2,1)S(1)}, bf16[2,192,2,128]{3,2,1,0:T(2,128)(2,1)S(1)}, u32[]{:S(2)}, u32[]{:S(2)}) collective-permute-start(bf16[2,192,2,128]{3,2,1,0:T(2,128)(2,1)S(1)} %pad_maximum_fusion.1), channel_id=1, source_target_pairs={{40,0},{48,8},{56,16},{64,24},{72,32},{80,40},{88,48},{96,56},{104... | collective-permute-start | bytes 589832 | tf_op jit(solution)/shard_map/ppermute | solution.py:17
  655.9 28.1 %collective-permute-start.28 = (bf16[2,192,2,128]{3,2,1,0:T(2,128)(2,1)S(1)}, bf16[2,192,2,128]{3,2,1,0:T(2,128)(2,1)S(1)}, u32[]{:S(2)}, u32[]{:S(2)}) collective-permute-start(bf16[2,192,2,128]{3,2,1,0:T(2,128)(2,1)S(1)} %pad_maximum_fusion.1), channel_id=1, source_target_pairs={{48,0},{56,8},{64,16},{72,24},{80,32},{88,40},{96,48},{104,56},{11... | collective-permute-start | bytes 589832 | tf_op jit(solution)/shard_map/ppermute | solution.py:17
  661.9 37.2 %collective-permute-start.29 = (bf16[2,192,2,128]{3,2,1,0:T(2,128)(2,1)S(1)}, bf16[2,192,2,128]{3,2,1,0:T(2,128)(2,1)S(1)}, u32[]{:S(2)}, u32[]{:S(2)}) collective-permute-start(bf16[2,192,2,128]{3,2,1,0:T(2,128)(2,1)S(1)} %pad_maximum_fusion.1), channel_id=1, source_target_pairs={{56,0},{64,8},{72,16},{80,24},{88,32},{96,40},{104,48},{112,56},{1... | collective-permute-start | bytes 589832 | tf_op jit(solution)/shard_map/ppermute | solution.py:17
  702.7 4.1 copy-start.1
Sparse Core Ops, SparseCore 0:
  51.9 71.4 all-gather.4
  125.5 126.3 all-gather.6
  254.0 138.6 all-gather.8
  411.9 80.8 reduce-scatter.2
  496.5 62.1 all-gather.10
  708.7 82.1 reduce-scatter.4
where the time goes:
time: 802 us; the launch traced here: 800 us
  waiting for transfers between devices  541 us (67%)
  starting transfers between devices  129 us (16%)
  blocking collectives  57.6 us (7%)
  between operations  23.3 us (3%)
  matrix products  18.5 us (2%)
  local copies, waits for them, and re-layouts  17.3 us (2%)
  other arithmetic  13 us (2%)
    ppermute x30, waiting for transfers between devices, from_behind(): return lax.ppermute(block, axis, route)  145 us
    reduce_scatter x2, waiting for transfers between devices, shards(): lax.psum_scatter(jnp.einsum('rc,dc->rd', attended, w_out, preferred_eleme...  133 us
    all_gather x2, waiting for transfers between devices, shards(): lax.all_gather(normed, 'space', axis=0, tiled=True)  133 us
    ppermute x30, starting transfers between devices, from_behind(): return lax.ppermute(block, axis, route)  129 us
    all_gather x1, waiting for transfers between devices, shards(): lax.all_gather(qkv_weight, 'queue', axis=1, tiled=True)  128 us
    all_gather x2, blocking collectives, shards(): mod_full = lax.all_gather(mod_part, 'space', axis=1, tiled=True)  57.6 us
  transfers between devices with their start and end apart: 36, of which 22 were waited for; matrix products, arithmetic and copies ran while one was open for 2% of the time, Pallas kernels for 0%

commit v1 on v0

v1 whole, which is shorter than its diff:
```python
import functools
import math

import jax
import jax.numpy as jnp
from jax import lax
from jax.experimental import pallas as pl
from jax.experimental.pallas import tpu as pltpu
from jax.sharding import PartitionSpec as P

MESH = pl.DeviceIdType.MESH
F32 = jnp.float32
BF16 = jnp.bfloat16
HEAD_DIM = 128
FREQ = 256
STEPS = 2
GROUPS = 3
HALF = 1536
SPACE = 8
FRAMES = 64


def kernel(
    hid, qkvw, outw, modw, omega, slot_frame, levels, timesteps,
    vel_out, lat_out,
    W, XS, MP, MG, MODF, G, LHS, KV, QS, ATT, PB, RB, VO,
    w_send, z_recv, x_recv, sib_recv, mod_send, mod_recv,
    ag_send, ag_recv, rs_send, rs_recv, kv_send, kv_recv, kvs_recv,
):
    q = lax.axis_index("queue")
    me = lax.axis_index("space")
    xl = q // 32
    z = (q % 32) // 2
    c = q % 2
    sib = q + 1 - 2 * c
    xp = (q + 32) % FRAMES

    def zq(d):
        return xl * 32 + ((z + d + 16) % 16) * 2 + c

    def xzq(d):
        return (1 - xl) * 32 + ((z + d + 16) % 16) * 2 + c

    up_q = (q + 2) % FRAMES
    down_q = (q + FRAMES - 2) % FRAMES
    peers = [(me + k) % SPACE for k in range(1, SPACE)]

    def send(src, dst, ss, rs, dev):
        pltpu.make_async_remote_copy(
            src_ref=src, dst_ref=dst, send_sem=ss, recv_sem=rs,
            device_id=dev, device_id_type=MESH,
        ).start()

    def wait(ref, sem):
        pltpu.make_async_copy(ref, ref, sem).wait()

    barrier = pltpu.get_barrier_semaphore()
    targets = [(zq(1), me), (zq(-1), me), (xp, me), (sib, me), (up_q, me), (down_q, me)]
    targets += [(q, p) for p in peers]
    for dev in targets:
        pl.semaphore_signal(barrier, inc=1, device_id=dev, device_id_type=MESH)

    W[q, 0] = qkvw[1]
    W[q, 1] = qkvw[2]
    W[q, 2] = qkvw[0]
    W[q, 3] = outw[...]

    frame = slot_frame[q]
    level = levels[frame]
    t_a = timesteps[level].astype(F32)
    t_b = timesteps[jnp.maximum(level - 1, 0)].astype(F32)
    t_c = timesteps[jnp.maximum(level - 2, 0)].astype(F32)
    dsigma = [(t_b - t_a) * (1.0 / 1000.0), (t_c - t_b) * (1.0 / 1000.0)]

    row = lax.broadcasted_iota(jnp.int32, (16, FREQ // 2), 0)
    angle = jnp.where(row % 2 == 0, t_a, t_b) * omega[...]
    emb = jnp.concatenate([jnp.cos(angle), jnp.sin(angle)], axis=-1).astype(BF16)
    cols = SPACE * 48
    part = [
        jnp.dot(emb, modw[k], preferred_element_type=F32)[:8] for k in range(3)
    ]
    prow = lax.broadcasted_iota(jnp.int32, (8, cols), 0)
    packed = jnp.where(prow < 2, part[0], jnp.where(prow < 4, part[1], part[2]))
    MP[...] = packed
    MG[me] = packed

    x = hid[0].astype(F32)
    for g in range(GROUPS):
        XS[g, 0] = x[8 * g : 8 * g + 8, :HALF]
        XS[g, 1] = x[8 * g : 8 * g + 8, HALF:]

    pl.semaphore_wait(barrier, len(targets))

    kv_half, qo_half = pl.ds(0, 2), pl.ds(2, 2)

    def w_move(idx, half, rs, dev):
        send(W.at[idx, half], W.at[idx, half], w_send, rs, dev)

    up, down = (zq(1), me), (zq(-1), me)
    xdev, sdev = (xp, me), (sib, me)
    w_move(q, kv_half, x_recv.at[16], xdev)
    w_move(q, kv_half, z_recv.at[0, 0, 0], up)
    w_move(q, kv_half, z_recv.at[1, 0, 0], down)
    w_move(q, qo_half, z_recv.at[0, 0, 2], up)
    w_move(q, qo_half, z_recv.at[1, 0, 2], down)
    w_move(q, kv_half, sib_recv.at[0], sdev)
    for p in peers:
        send(MP, MG.at[me], mod_send, mod_recv, (q, p))
    w_move(q, qo_half, x_recv.at[0], xdev)
    w_move(q, qo_half, sib_recv.at[1], sdev)

    wait(W.at[xp, kv_half], x_recv.at[16])
    w_move(xp, kv_half, z_recv.at[0, 0, 1], up)
    w_move(xp, kv_half, z_recv.at[1, 0, 1], down)
    w_move(xp, kv_half, sib_recv.at[0], sdev)

    def relay(h, way):
        d = -h if way == 0 else h
        onward = up if way == 0 else down
        own, other = zq(d), xzq(d)
        last = h == 8
        for m in (0, 1, 2):
            if last and ((m == 1) == (way == 0)):
                continue
            idx = other if m == 1 else own
            half = qo_half if m == 2 else kv_half
            wait(W.at[idx, half], z_recv.at[way, h - 1, m])
            more = h < 7 or (h == 7 and (m == 1) == (way == 1))
            if more:
                w_move(idx, half, z_recv.at[way, h, m], onward)
            if m == 2:
                w_move(idx, half, x_recv.at[h if way == 0 else 8 + h], xdev)
            w_move(idx, half, sib_recv.at[1 if m == 2 else 0], sdev)

    def take_x(j):
        idx = xp if j == 0 else (xzq(-j) if j <= 8 else xzq(j - 8))
        wait(W.at[idx, qo_half], x_recv.at[j])
        w_move(idx, qo_half, sib_recv.at[1], sdev)

    def spread_modulation():
        wait(MG.at[pl.ds(0, SPACE - 1)], mod_recv)
        for st in range(STEPS):
            for k in range(3):
                r = 2 * k + st
                for half in range(2):
                    vec = jnp.concatenate(
                        [MG[4 * half + j, r : r + 1, :] for j in range(4)], axis=-1
                    )
                    if k == 1:
                        vec = vec + 1.0
                    MODF[st, k, half] = jnp.broadcast_to(vec, (8, HALF))

    def norm_send(st, g):
        left, right = XS[g, 0], XS[g, 1]
        mean = (
            jnp.sum(left, axis=-1, keepdims=True) + jnp.sum(right, axis=-1, keepdims=True)
        ) * (1.0 / (2 * HALF))
        left, right = left - mean, right - mean
        var = (
            jnp.sum(left * left, axis=-1, keepdims=True)
            + jnp.sum(right * right, axis=-1, keepdims=True)
        ) * (1.0 / (2 * HALF))
        inv = 1.0 / jnp.sqrt(var + 1e-6)
        left = left * inv * MODF[st, 1, 0] + MODF[st, 0, 0]
        right = right * inv * MODF[st, 1, 1] + MODF[st, 0, 1]
        G[st, g, me] = jnp.concatenate([left, right], axis=0).astype(BF16)
        for p in peers:
            send(G.at[st, g, me], G.at[st, g, me], ag_send.at[st, g], ag_recv.at[st, g], (q, p))

    def rms(values):
        parts = []
        for h in range(2):
            wide = values[:, h * HEAD_DIM : (h + 1) * HEAD_DIM]
            mean = jnp.mean(wide * wide, axis=-1, keepdims=True)
            parts.append(wide * (1.0 / jnp.sqrt(mean + 1e-6)))
        return jnp.concatenate(parts, axis=-1)

    def project(g, part_index):
        acc = None
        for j in range(4):
            term = jnp.dot(
                LHS[g, :, 768 * j : 768 * (j + 1)],
                W[16 * j : 16 * (j + 1), part_index].reshape(768, 256),
                preferred_element_type=F32,
            )
            acc = term if acc is None else acc + term
        return acc.astype(BF16)

    def kv_move(st, g, w, rs, dev, to):
        send(KV.at[st, g, w], KV.at[st, g, to], kv_send.at[st, g], rs, dev)

    def sib_kv(st, g, w):
        to = w + 2 * c - 1
        kv_move(st, g, w, kvs_recv.at[st, g, to], sdev, to)

    kv_up, kv_down = (up_q, me), (down_q, me)

    def take_rows(st, g):
        wait(G.at[st, g, pl.ds(0, SPACE - 1)], ag_recv.at[st, g])
        rows = G[st, g].astype(F32)
        LHS[g, :, :HALF] = rows[:, :8].reshape(64, HALF).astype(BF16)
        LHS[g, :, HALF:] = rows[:, 8:].reshape(64, HALF).astype(BF16)

    def project_kv(st, g):
        KV[st, g, 8, 0] = rms(project(g, 0).astype(F32)).astype(BF16)
        KV[st, g, 8, 1] = project(g, 1)
        kv_move(st, g, 8, kv_recv.at[st, g, 3], kv_up, 6)
        kv_move(st, g, 8, kv_recv.at[st, g, 5], kv_down, 10)
        sib_kv(st, g, 8)

    def project_q(st, g):
        hat = rms(project(g, 2).astype(F32)).astype(BF16).astype(F32)
        QS[g] = hat * (1.0 / math.sqrt(HEAD_DIM))

    def kv_relay(st, g, h):
        lo, hi = 8 - 2 * h, 8 + 2 * h
        wait(KV.at[st, g, lo], kv_recv.at[st, g, lo // 2])
        if h < 4:
            kv_move(st, g, lo, kv_recv.at[st, g, lo // 2 - 1], kv_up, lo - 2)
            sib_kv(st, g, lo)
            wait(KV.at[st, g, hi], kv_recv.at[st, g, hi // 2])
            if h < 3:
                kv_move(st, g, hi, kv_recv.at[st, g, hi // 2 + 1], kv_down, hi + 2)
            else:

                @pl.when(c == 0)
                def _():
                    kv_move(st, g, hi, kv_recv.at[st, g, hi // 2 + 1], kv_down, hi + 2)

            sib_kv(st, g, hi)
        else:

            @pl.when(c == 0)
            def _():
                wait(KV.at[st, g, hi], kv_recv.at[st, g, hi // 2])
                sib_kv(st, g, hi)

            @pl.when(c == 1)
            def _():
                sib_kv(st, g, lo)

    masks = []
    for w in range(16):
        f = frame + (w - 8)
        masks.append(jnp.where((f >= 0) & (f < FRAMES), 1.0, 0.0).astype(F32))

    def attend(st, g):
        for w in range(1, 16, 2):
            wait(KV.at[st, g, w], kvs_recv.at[st, g, w])

        def rows16(i, carry):
            at = pl.ds(pl.multiple_of(i * 16, 16), 16)
            for h in range(2):
                lanes = pl.ds(h * HEAD_DIM, HEAD_DIM)
                query = QS[g, at, lanes]
                num = jnp.zeros((16, HEAD_DIM), F32)
                den = jnp.zeros((16, 1), F32)
                for w in range(16):
                    key = KV[st, g, w, 0, at, lanes].astype(F32)
                    score = jnp.sum(query * key, axis=-1, keepdims=True)
                    e = jnp.exp(score) * masks[w]
                    den = den + e
                    num = num + e * KV[st, g, w, 1, at, lanes].astype(F32)
                ATT[g, at, lanes] = (num / den).astype(BF16)
            return carry

        lax.fori_loop(0, 4, rows16, 0)

    def out_send(st, g):
        for j in range(2):
            pair = []
            for half in range(2):
                k = j + 2 * half
                pair.append(
                    lax.dot_general(
                        ATT[g],
                        W[16 * k : 16 * (k + 1), 3].reshape(768, 256),
                        (((1,), (1,)), ((), ())),
                        preferred_element_type=F32,
                    ).reshape(8, 8, 768)
                )
            PB[st, g, :, :, 768 * j : 768 * (j + 1)] = jnp.concatenate(pair, axis=1).astype(BF16)
        RB[st, g, me] = PB[st, g, me]
        for p in peers:
            send(PB.at[st, g, p], RB.at[st, g, me], rs_send.at[st, g], rs_recv.at[st, g], (q, p))

    def update(st, g):
        wait(RB.at[st, g, pl.ds(0, SPACE - 1)], rs_recv.at[st, g])
        branch = jnp.sum(RB[st, g].astype(F32), axis=0)
        for half in range(2):
            cur = XS[g, half]
            vel = cur + MODF[st, 2, half] * branch[8 * half : 8 * half + 8]
            VO[st, 8 * g : 8 * g + 8, half * HALF : (half + 1) * HALF] = vel
            XS[g, half] = (cur + dsigma[st] * vel).astype(BF16).astype(F32)

    spread_modulation()
    for g in range(GROUPS):
        norm_send(0, g)
    for h in range(1, 9):
        relay(h, 0)
        relay(h, 1)
        if h == 1:
            take_x(0)
        else:
            take_x(h - 1)
            take_x(8 + h - 1)
    take_x(8)
    wait(W.at[pl.ds(0, 32), kv_half], sib_recv.at[0])
    wait(W.at[pl.ds(0, 32), qo_half], sib_recv.at[1])

    for st in range(STEPS):
        for g in range(GROUPS):
            take_rows(st, g)
            project_kv(st, g)
        for g in range(GROUPS):
            project_q(st, g)
        for h in range(1, 4):
            for g in range(GROUPS):
                kv_relay(st, g, h)
        kv_relay(st, 0, 4)
        kv_relay(st, 1, 4)
        attend(st, 0)
        out_send(st, 0)
        kv_relay(st, 2, 4)
        attend(st, 1)
        out_send(st, 1)
        attend(st, 2)
        out_send(st, 2)
        for g in range(GROUPS):
            update(st, g)
            if st + 1 < STEPS:
                norm_send(st + 1, g)

    for st in range(STEPS):
        vel_out[st, 0] = VO[st].astype(BF16)
    for g in range(GROUPS):
        for half in range(2):
            VO[0, 8 * g : 8 * g + 8, half * HALF : (half + 1) * HALF] = XS[g, half]
    lat_out[0] = VO[0].astype(BF16)

    wait(W.at[pl.ds(0, 63)], w_send)
    wait(MG.at[pl.ds(0, SPACE - 1)], mod_send)
    for st in range(STEPS):
        for g in range(GROUPS):
            wait(G.at[st, g, pl.ds(0, SPACE - 1)], ag_send.at[st, g])
            wait(RB.at[st, g, pl.ds(0, SPACE - 1)], rs_send.at[st, g])

            @pl.when(c == 0)
            def _():
                wait(KV.at[st, g, pl.ds(0, 16)], kv_send.at[st, g])

            @pl.when(c == 1)
            def _():
                wait(KV.at[st, g, pl.ds(0, 15)], kv_send.at[st, g])


def shards(hidden, qkv_weight, out_weight, mod_weight, slot_frame, levels, timesteps):
    half_freq = FREQ // 2
    omega = jnp.exp(-math.log(10000.0) * jnp.arange(half_freq).astype(F32) / half_freq)
    vmem = pl.BlockSpec(memory_space=pltpu.VMEM)
    smem = pl.BlockSpec(memory_space=pltpu.SMEM)
    dma = pltpu.SemaphoreType.DMA
    width = SPACE * 48
    return pl.pallas_call(
        kernel,
        name="denoise",
        out_shape=(
            jax.ShapeDtypeStruct((STEPS, 1, 24, 2 * HALF), BF16),
            jax.ShapeDtypeStruct((1, 24, 2 * HALF), BF16),
        ),
        in_specs=[vmem] * 5 + [smem] * 3,
        out_specs=(vmem, vmem),
        scratch_shapes=[
            pltpu.VMEM((FRAMES, 4, 48, 256), BF16),
            pltpu.VMEM((GROUPS, 2, 8, HALF), F32),
            pltpu.VMEM((8, width), F32),
            pltpu.VMEM((SPACE, 8, width), F32),
            pltpu.VMEM((STEPS, 3, 2, 8, HALF), F32),
            pltpu.VMEM((STEPS, GROUPS, SPACE, 16, HALF), BF16),
            pltpu.VMEM((GROUPS, 64, 2 * HALF), BF16),
            pltpu.VMEM((STEPS, GROUPS, 17, 2, 64, 256), BF16),
            pltpu.VMEM((GROUPS, 64, 256), F32),
            pltpu.VMEM((GROUPS, 64, 256), BF16),
            pltpu.VMEM((STEPS, GROUPS, SPACE, 16, HALF), BF16),
            pltpu.VMEM((STEPS, GROUPS, SPACE, 16, HALF), BF16),
            pltpu.VMEM((STEPS, 24, 2 * HALF), F32),
            dma,
            dma((2, 8, 3)),
            dma((17,)),
            dma((2,)),
            dma,
            dma,
            dma((STEPS, GROUPS)),
            dma((STEPS, GROUPS)),
            dma((STEPS, GROUPS)),
            dma((STEPS, GROUPS)),
            dma((STEPS, GROUPS)),
            dma((STEPS, GROUPS, 9)),
            dma((STEPS, GROUPS, 16)),
        ],
        compiler_params=pltpu.CompilerParams(
            collective_id=0, has_side_effects=True, vmem_limit_bytes=48 * 1024 * 1024
        ),
    )(
        hidden, qkv_weight, out_weight, jnp.transpose(mod_weight, (1, 0, 2)), omega[None],
        slot_frame, levels, timesteps,
    )


def solution(mesh):
    in_specs = (
        P("queue", "space", None),
        P(None, "queue", "space"),
        P("queue", "space"),
        P(None, None, "space"),
        P(),
        P(),
        P(),
    )
    out_specs = (P(None, "queue", "space", None), P("queue", "space", None))
    return jax.shard_map(shards, mesh=mesh, in_specs=in_specs, out_specs=out_specs, check_vma=False)
```

time: 802 us -> 155 us (0.19)
  waiting for transfers between devices: 541 us -> 0 us
  Pallas kernels: 0 us -> 149 us
  starting transfers between devices: 129 us -> 0 us
  blocking collectives: 57.6 us -> 0 us
  between operations: 23.3 us -> 0.67 us
  matrix products: 18.5 us -> 0 us
  other arithmetic: 13 us -> 0.01 us
  local copies, waits for them, and re-layouts: 17.3 us -> 5.62 us
    all_gather x4 -> x0, waiting for transfers between devices: 261 us -> none  [the longest x2 133 us: shards(): lax.all_gather(normed, 'space', axis=0, tiled=True)]
    pallas_call x0 -> x1, Pallas kernels: none -> 149 us  [shards(): pl.pallas_call(kernel, name='denoise', out_shape=(jax.ShapeDtypeStruct((S...]
    ppermute x30 -> x0, waiting for transfers between devices: 145 us -> none  [from_behind(): return lax.ppermute(block, axis, route)]
    reduce_scatter x2 -> x0, waiting for transfers between devices: 133 us -> none  [shards(): lax.psum_scatter(jnp.einsum('rc,dc->rd', attended, w_out, preferred_eleme...]
    ppermute x30 -> x0, starting transfers between devices: 129 us -> none  [from_behind(): return lax.ppermute(block, axis, route)]
    all_gather x2 -> x0, blocking collectives: 57.6 us -> none  [shards(): mod_full = lax.all_gather(mod_part, 'space', axis=1, tiled=True)]
    dot_general x10 -> x0, matrix products: 18.5 us -> none  [the longest x2 7.57 us: shards(): jnp.einsum('rd,kdc->rkc', lax.all_gather(normed, 'space', axis=0, tiled=T...]
  transfers between devices with their start and end apart: 36 -> 0, of which waited for: 22 -> 0; matrix products, arithmetic and copies ran while one was open for 2% -> 0% of each run, Pallas kernels for 0% -> 0%
where the time goes in v1:
time: 155 us
  Pallas kernels  149 us (96%)
  local copies, waits for them, and re-layouts  5.62 us (4%)
    pallas_call x1, Pallas kernels, shards(): pl.pallas_call(kernel, name='denoise', out_shape=(jax.ShapeDtypeStruct((S...  149 us
    unnamed x16, local copies, waits for them, and re-layouts  5.62 us

profile of v1, /device:TPU:1, one launch (start us, length us, event | category | flops | bytes accessed | tf_op | source)
XLA Modules:
  0.0 155.0 jit_solution(7887769690395473513)
XLA Ops:
  0.6 0.0 copy-start.4
  0.6 0.0 copy-start.5
  0.7 0.0 copy-start.6
  0.7 0.6 copy-done.4
  1.3 0.0 copy-done.5
  1.3 0.0 copy-done.6
  1.3 0.0 copy-start
  1.3 1.1 copy-done
  2.4 0.0 copy-start.1
  2.4 0.9 copy-done.1
  3.3 0.0 copy-start.2
  3.3 0.9 copy-done.2
  4.2 0.0 copy-start.3
  4.2 0.7 copy-done.3
  4.9 148.7 %denoise.1 = (bf16[2,1,24,3072]{3,2,1,0:T(8,128)(2,1)S(1)}, bf16[1,24,3072]{2,1,0:T(8,128)(2,1)S(1)}) custom-call(bf16[1,24,3072]{2,1,0:T(8,128)(2,1)S(1)} %copy-done.1, bf16[3,48,256]{2,1,0:T(8,128)(2,1)S(1)} %copy-done.2, bf16[48,256]{1,0:T(8,128)(2,1)S(1)} %copy-done.3, bf16[3,256,384]{2,1,0:T(8,128)(2,1)S(1)} %bitcast.1, ...), custom_call_target="tpu_custom_call" | custom-call | tf_op jit(solution)/shard_map/denoise/pallas_call | solution.py:364
  153.7 0.7 copy.11
  154.4 0.7 copy.12
  (1 shorter events, 0.0 us)
Async XLA Ops:
  0.6 0.7 copy-start.4
  0.6 0.7 copy-start.5
  0.7 0.7 copy-start.6
  1.3 1.1 copy-start
  2.4 0.9 copy-start.1
  3.3 0.9 copy-start.2
  4.2 0.7 copy-start.3

commit v2 on v1

v2 whole, which is shorter than its diff:
```python
import functools
import math

import jax
import jax.numpy as jnp
from jax import lax
from jax.experimental import pallas as pl
from jax.experimental.pallas import tpu as pltpu
from jax.sharding import PartitionSpec as P

MESH = pl.DeviceIdType.MESH
F32 = jnp.float32
BF16 = jnp.bfloat16
HEAD_DIM = 128
FREQ = 256
STEPS = 2
GROUPS = 3
HALF = 1536
SPACE = 8
FRAMES = 64


def kernel(
    hid, qkvw, outw, modw, omega, slot_frame, levels, timesteps,
    vel_out, lat_out,
    W, WX, XS, MP, MG, MODF, G, LHS, KV, QS, ATT, ATX, PB, RB, VO, HS, MW, in_sem,
    w_send, z_recv, x_recv, sib_recv, wx_send, wx_recv, mod_send, mod_recv,
    ag_send, ag_recv, agx_recv, agy_recv, at_send, at_recv, rs_send, rs_recv,
    kv_send, kv_recv, kvs_recv,
):
    q = lax.axis_index("queue")
    me = lax.axis_index("space")
    xl = q // 32
    z = (q % 32) // 2
    c = q % 2
    y, xh = me // 2, me % 2
    slot = xh * 4 + y
    sib = q + 1 - 2 * c
    xp = (q + 32) % FRAMES

    def zq(d):
        return xl * 32 + ((z + d + 16) % 16) * 2 + c

    def xzq(d):
        return (1 - xl) * 32 + ((z + d + 16) % 16) * 2 + c

    up_q = (q + 2) % FRAMES
    down_q = (q + FRAMES - 2) % FRAMES
    peers = [(me + k) % SPACE for k in range(1, SPACE)]
    ydevs = [(q, (me + 2 * k) % SPACE) for k in (1, 3, 2)]
    hdev = (q, me + 1 - 2 * xh)
    odev = (xp, me + 1 - 2 * xh)
    kv_up, kv_down = (up_q, me), (down_q, me)
    up, down = (zq(1), me), (zq(-1), me)
    xdev, sdev = (xp, me), (sib, me)

    def send(src, dst, ss, rs, dev):
        pltpu.make_async_remote_copy(
            src_ref=src, dst_ref=dst, send_sem=ss, recv_sem=rs,
            device_id=dev, device_id_type=MESH,
        ).start()

    def wait(ref, sem):
        pltpu.make_async_copy(ref, ref, sem).wait()

    barrier = pltpu.get_barrier_semaphore()
    targets = [up, down, xdev, sdev, odev, kv_up, kv_down] + [(q, p) for p in peers]
    for dev in targets:
        pl.semaphore_signal(barrier, inc=1, device_id=dev, device_id_type=MESH)

    loads = [
        pltpu.make_async_copy(qkvw.at[pl.ds(1, 2)], W.at[q // 2, c, pl.ds(0, 2)], in_sem.at[0]),
        pltpu.make_async_copy(qkvw.at[0], W.at[q // 2, c, 2], in_sem.at[1]),
        pltpu.make_async_copy(outw, W.at[q // 2, c, 3], in_sem.at[2]),
        pltpu.make_async_copy(modw, MW, in_sem.at[3]),
        pltpu.make_async_copy(hid.at[0], HS, in_sem.at[4]),
    ]
    for load in loads:
        load.start()

    kv_half, qo_half = pl.ds(0, 2), pl.ds(2, 2)

    def w_move(idx, half, rs, dev):
        ref = W.at[idx // 2, c, half]
        send(ref, ref, w_send.at[1 if dev is sdev else 0], rs, dev)

    def w_wait(idx, half, sem):
        wait(W.at[idx // 2, c, half], sem)

    def z_move(idx, k, h, way, m):
        w_move(idx, k, z_recv.at[way, h, m], down if way else up)

    for load in loads[:3]:
        load.wait()
    pl.semaphore_wait(barrier, len(targets))
    z_move(q, 0, 0, 0, 0)
    z_move(q, 0, 0, 1, 0)
    w_move(q, kv_half, x_recv.at[16], xdev)
    z_move(q, 1, 0, 0, 1)
    z_move(q, 1, 0, 1, 1)
    for k in (2, 3):
        z_move(q, k, 0, 0, k + 2)
        z_move(q, k, 0, 1, k + 2)
    w_move(q, qo_half, x_recv.at[0], xdev)
    w_move(q, kv_half, sib_recv.at[0], sdev)
    w_move(q, qo_half, sib_recv.at[1], sdev)

    frame = slot_frame[q]
    level = levels[frame]
    t_a = timesteps[level].astype(F32)
    t_b = timesteps[jnp.maximum(level - 1, 0)].astype(F32)
    t_c = timesteps[jnp.maximum(level - 2, 0)].astype(F32)
    dsigma = [(t_b - t_a) * (1.0 / 1000.0), (t_c - t_b) * (1.0 / 1000.0)]

    row = lax.broadcasted_iota(jnp.int32, (16, FREQ // 2), 0)
    angle = jnp.where(row % 2 == 0, t_a, t_b) * omega[...]
    emb = jnp.concatenate([jnp.cos(angle), jnp.sin(angle)], axis=-1).astype(BF16)
    cols = SPACE * 48
    loads[3].wait()
    part = [
        jnp.dot(emb, MW[k], preferred_element_type=F32)[:8] for k in range(3)
    ]
    prow = lax.broadcasted_iota(jnp.int32, (8, cols), 0)
    packed = jnp.where(prow < 2, part[0], jnp.where(prow < 4, part[1], part[2]))
    MP[...] = packed
    MG[me] = packed
    for p in peers:
        send(MP, MG.at[me], mod_send, mod_recv, (q, p))

    loads[4].wait()
    x = HS[...].astype(F32)
    for g in range(GROUPS):
        XS[g, 0] = x[8 * g : 8 * g + 8, :HALF]
        XS[g, 1] = x[8 * g : 8 * g + 8, HALF:]

    def seed():
        w_wait(xp, kv_half, x_recv.at[16])
        for k in (0, 1):
            z_move(xp, k, 0, 0, k + 2)
            z_move(xp, k, 0, 1, k + 2)
        w_move(xp, kv_half, sib_recv.at[0], sdev)

    def relay(h, way, m):
        theirs = m in (2, 3)
        if h == 8 and theirs == (way == 0):
            return
        d = -h if way == 0 else h
        idx = xzq(d) if theirs else zq(d)
        k = (0, 1, 0, 1, 2, 3)[m]
        w_wait(idx, k, z_recv.at[way, h - 1, m])
        if h < 7 or (h == 7 and theirs == (way == 1)):
            z_move(idx, k, h, way, m)
        if m % 2 == 1:
            half = qo_half if m == 5 else kv_half
            if m == 5:
                w_move(idx, half, x_recv.at[h if way == 0 else 8 + h], xdev)
            w_move(idx, half, sib_recv.at[1 if m == 5 else 0], sdev)

    def take_x(j):
        idx = xp if j == 0 else (xzq(-j) if j <= 8 else xzq(j - 8))
        w_wait(idx, qo_half, x_recv.at[j])
        w_move(idx, qo_half, sib_recv.at[1], sdev)

    def finish_weights():
        wait(W.at[pl.ds(0, 16), pl.ds(0, 2), qo_half], sib_recv.at[1])

    def partner_weights():
        send(W.at[pl.ds(0, 32), c, 3], WX.at[pl.ds(0, 32), c], wx_send.at[0], wx_recv.at[0], odev)

    def share_partner_weights():
        own = WX.at[pl.ds(0, 32), c]
        wait(own, wx_recv.at[0])
        send(own, own, wx_send.at[1], wx_recv.at[1], sdev)

    def finish_partner_weights():
        wait(WX.at[pl.ds(0, 32), c], wx_recv.at[1])

    def spread_modulation():
        wait(MG.at[pl.ds(0, SPACE - 1)], mod_recv)
        for st in range(STEPS):
            for k in range(3):
                r = 2 * k + st
                for half in range(2):
                    vec = jnp.concatenate(
                        [MG[4 * half + j, r : r + 1, :] for j in range(4)], axis=-1
                    )
                    if k == 1:
                        vec = vec + 1.0
                    MODF[st, k, half] = jnp.broadcast_to(vec, (8, HALF))

    def g_move(st, g, at, rs, dev):
        ref = G.at[st, g, at]
        send(ref, ref, ag_send.at[st, g], rs, dev)

    def norm_send(st, g):
        left, right = XS[g, 0], XS[g, 1]
        mean = (
            jnp.sum(left, axis=-1, keepdims=True) + jnp.sum(right, axis=-1, keepdims=True)
        ) * (1.0 / (2 * HALF))
        left, right = left - mean, right - mean
        var = (
            jnp.sum(left * left, axis=-1, keepdims=True)
            + jnp.sum(right * right, axis=-1, keepdims=True)
        ) * (1.0 / (2 * HALF))
        inv = 1.0 / jnp.sqrt(var + 1e-6)
        left = left * inv * MODF[st, 1, 0] + MODF[st, 0, 0]
        right = right * inv * MODF[st, 1, 1] + MODF[st, 0, 1]
        G[st, g, slot] = jnp.concatenate([left, right], axis=0).astype(BF16)
        g_move(st, g, slot, agx_recv.at[st, g], hdev)
        g_move(st, g, slot, ag_recv.at[st, g], ydevs[0])
        g_move(st, g, slot, ag_recv.at[st, g], ydevs[1])
        g_move(st, g, slot, agy_recv.at[st, g], ydevs[2])

    def norm_pass(st, g):
        other = (1 - xh) * 4 + y
        wait(G.at[st, g, other], agx_recv.at[st, g])
        g_move(st, g, other, ag_recv.at[st, g], ydevs[0])
        g_move(st, g, other, ag_recv.at[st, g], ydevs[1])
        far = xh * 4 + (y + 2) % 4
        wait(G.at[st, g, far], agy_recv.at[st, g])
        g_move(st, g, far, ag_recv.at[st, g], hdev)

    def rms(values):
        parts = []
        for h in range(2):
            wide = values[:, h * HEAD_DIM : (h + 1) * HEAD_DIM]
            mean = jnp.mean(wide * wide, axis=-1, keepdims=True)
            parts.append(wide * (1.0 / jnp.sqrt(mean + 1e-6)))
        return jnp.concatenate(parts, axis=-1)

    def project(g, part_index):
        acc = None
        for j in range(4):
            term = jnp.dot(
                LHS[g, :, 768 * j : 768 * (j + 1)],
                W[8 * j : 8 * (j + 1), :, part_index].reshape(768, 256),
                preferred_element_type=F32,
            )
            acc = term if acc is None else acc + term
        return acc.astype(BF16)

    def kv_move(st, g, w, k, rs, dev, to):
        send(KV.at[st, g, w, k], KV.at[st, g, to, k], kv_send.at[st, g], rs, dev)

    def kv_pass(st, g, w, k, way):
        to = w + 2 if way else w - 2
        kv_move(st, g, w, k, kv_recv.at[st, g, to // 2, k], kv_down if way else kv_up, to)

    def kv_wait(st, g, w, k):
        wait(KV.at[st, g, w, k], kv_recv.at[st, g, w // 2, k])

    def sib_kv(st, g, w):
        to = w + 2 * c - 1
        send(KV.at[st, g, w], KV.at[st, g, to], kv_send.at[st, g], kvs_recv.at[st, g, to], sdev)

    def take_rows(st, g):
        wait(G.at[st, g, pl.ds(0, 5)], ag_recv.at[st, g])
        rows = G[st, g].astype(F32)
        LHS[g, :, :HALF] = rows[:, :8].reshape(64, HALF).astype(BF16)
        LHS[g, :, HALF:] = rows[:, 8:].reshape(64, HALF).astype(BF16)

    def project_kv(st, g):
        KV[st, g, 8, 0] = rms(project(g, 0).astype(F32)).astype(BF16)
        kv_pass(st, g, 8, 0, 0)
        kv_pass(st, g, 8, 0, 1)
        KV[st, g, 8, 1] = project(g, 1)
        kv_pass(st, g, 8, 1, 0)
        kv_pass(st, g, 8, 1, 1)
        sib_kv(st, g, 8)

    def project_q(st, g):
        hat = rms(project(g, 2).astype(F32)).astype(BF16).astype(F32)
        QS[g] = hat * (1.0 / math.sqrt(HEAD_DIM))

    def kv_relay(st, g, h):
        lo, hi = 8 - 2 * h, 8 + 2 * h
        if h < 4:
            for k in range(2):
                kv_wait(st, g, lo, k)
                kv_pass(st, g, lo, k, 0)
                kv_wait(st, g, hi, k)
                if h < 3:
                    kv_pass(st, g, hi, k, 1)
                else:

                    @pl.when(c == 0)
                    def _():
                        kv_pass(st, g, hi, k, 1)

            sib_kv(st, g, lo)
            sib_kv(st, g, hi)
        else:
            kv_wait(st, g, lo, 0)
            kv_wait(st, g, lo, 1)

            @pl.when(c == 0)
            def _():
                kv_wait(st, g, hi, 0)
                kv_wait(st, g, hi, 1)
                sib_kv(st, g, hi)

            @pl.when(c == 1)
            def _():
                sib_kv(st, g, lo)

    masks = []
    for w in range(16):
        f = frame + (w - 8)
        masks.append(jnp.where((f >= 0) & (f < FRAMES), 1.0, 0.0).astype(F32))

    def attend(st, g):
        for w in range(1, 16, 2):
            wait(KV.at[st, g, w], kvs_recv.at[st, g, w])

        def rows16(i, carry):
            at = pl.ds(pl.multiple_of(i * 16, 16), 16)
            for h in range(2):
                lanes = pl.ds(h * HEAD_DIM, HEAD_DIM)
                query = QS[g, at, lanes]
                num = jnp.zeros((16, HEAD_DIM), F32)
                den = jnp.zeros((16, 1), F32)
                for w in range(16):
                    key = KV[st, g, w, 0, at, lanes].astype(F32)
                    score = jnp.sum(query * key, axis=-1, keepdims=True)
                    e = jnp.exp(score) * masks[w]
                    den = den + e
                    num = num + e * KV[st, g, w, 1, at, lanes].astype(F32)
                ATT[st, g, i // 2, pl.ds(pl.multiple_of((i % 2) * 16, 16), 16), lanes] = (
                    num / den
                ).astype(BF16)
            return carry

        lax.fori_loop(0, 4, rows16, 0)
        send(ATT.at[st, g, 1 - xh], ATX.at[st, g], at_send.at[st, g], at_recv.at[st, g], hdev)

    def out_send(st, g):
        wait(ATX.at[st, g], at_recv.at[st, g])
        own, other = ATT[st, g, xh], ATX[st, g]
        for j in range(2):
            pair = []
            for half in range(2):
                k = j + 2 * half
                total = None
                for rows, weight in (
                    (own, W[8 * k : 8 * (k + 1), :, 3]), (other, WX[8 * k : 8 * (k + 1)])
                ):
                    term = lax.dot_general(
                        rows, weight.reshape(768, 256), (((1,), (1,)), ((), ())),
                        preferred_element_type=F32,
                    )
                    total = term if total is None else total + term
                pair.append(total.reshape(4, 8, 768))
            PB[st, g, :, :, 768 * j : 768 * (j + 1)] = jnp.concatenate(pair, axis=1).astype(BF16)
        RB[st, g, y] = PB[st, g, y]
        for k, dev in zip((1, 3, 2), ydevs):
            send(
                PB.at[st, g, (y + k) % 4], RB.at[st, g, y],
                rs_send.at[st, g], rs_recv.at[st, g], dev,
            )

    def update(st, g):
        wait(RB.at[st, g, pl.ds(0, 3)], rs_recv.at[st, g])
        branch = jnp.sum(RB[st, g].astype(F32), axis=0)
        for half in range(2):
            cur = XS[g, half]
            vel = cur + MODF[st, 2, half] * branch[8 * half : 8 * half + 8]
            VO[st, 8 * g : 8 * g + 8, half * HALF : (half + 1) * HALF] = vel
            XS[g, half] = (cur + dsigma[st] * vel).astype(BF16).astype(F32)

    for h in range(1, 9):
        for m in range(6):
            relay(h, 0, m)
            relay(h, 1, m)
            if h == 1 and m == 1:
                seed()
        if h == 1:
            take_x(0)
            spread_modulation()
        else:
            take_x(h - 1)
            take_x(8 + h - 1)
        if 2 <= h <= 4:
            norm_send(0, h - 2)
        if 5 <= h <= 7:
            norm_pass(0, h - 5)
    take_x(8)
    partner_weights()
    wait(W.at[pl.ds(0, 16), pl.ds(0, 2), kv_half], sib_recv.at[0])

    for st in range(STEPS):
        for g in range(GROUPS):
            take_rows(st, g)
            project_kv(st, g)
        if st == 0:
            finish_weights()
        for g in range(GROUPS):
            project_q(st, g)
        for h in range(1, 4):
            for g in range(GROUPS):
                kv_relay(st, g, h)
        if st == 0:
            share_partner_weights()
        else:
            vel_out[0, 0] = VO[0].astype(BF16)
        kv_relay(st, 0, 4)
        kv_relay(st, 1, 4)
        attend(st, 0)
        kv_relay(st, 2, 4)
        attend(st, 1)
        if st == 0:
            finish_partner_weights()
        out_send(st, 0)
        attend(st, 2)
        out_send(st, 1)
        out_send(st, 2)
        for g in range(GROUPS):
            update(st, g)
            if st + 1 < STEPS:
                norm_send(st + 1, g)
                if g > 0:
                    norm_pass(st + 1, g - 1)
        if st + 1 < STEPS:
            norm_pass(st + 1, GROUPS - 1)

    vel_out[1, 0] = VO[1].astype(BF16)
    for g in range(GROUPS):
        for half in range(2):
            VO[0, 8 * g : 8 * g + 8, half * HALF : (half + 1) * HALF] = XS[g, half]
    lat_out[0] = VO[0].astype(BF16)

    wait(W.at[pl.ds(0, 31), 0], w_send.at[0])
    wait(W.at[pl.ds(0, 16)], w_send.at[1])
    for k in range(2):
        wait(WX.at[pl.ds(0, 32), c], wx_send.at[k])
    wait(MG.at[pl.ds(0, SPACE - 1)], mod_send)
    for st in range(STEPS):
        for g in range(GROUPS):
            wait(G.at[st, g, pl.ds(0, SPACE - 1)], ag_send.at[st, g])
            wait(ATX.at[st, g], at_send.at[st, g])
            wait(RB.at[st, g, pl.ds(0, 3)], rs_send.at[st, g])

            @pl.when(c == 0)
            def _():
                wait(KV.at[st, g, pl.ds(0, 16)], kv_send.at[st, g])

            @pl.when(c == 1)
            def _():
                wait(KV.at[st, g, pl.ds(0, 15)], kv_send.at[st, g])


def shards(hidden, qkv_weight, out_weight, mod_weight, slot_frame, levels, timesteps):
    half_freq = FREQ // 2
    omega = jnp.exp(-math.log(10000.0) * jnp.arange(half_freq).astype(F32) / half_freq)
    vmem = pl.BlockSpec(memory_space=pltpu.VMEM)
    hbm = pl.BlockSpec(memory_space=pltpu.HBM)
    smem = pl.BlockSpec(memory_space=pltpu.SMEM)
    dma = pltpu.SemaphoreType.DMA
    width = SPACE * 48
    return pl.pallas_call(
        kernel,
        name="denoise",
        out_shape=(
            jax.ShapeDtypeStruct((STEPS, 1, 24, 2 * HALF), BF16),
            jax.ShapeDtypeStruct((1, 24, 2 * HALF), BF16),
        ),
        in_specs=[hbm] * 4 + [vmem] + [smem] * 3,
        out_specs=(vmem, vmem),
        scratch_shapes=[
            pltpu.VMEM((FRAMES // 2, 2, 4, 48, 256), BF16),
            pltpu.VMEM((FRAMES // 2, 2, 48, 256), BF16),
            pltpu.VMEM((GROUPS, 2, 8, HALF), F32),
            pltpu.VMEM((8, width), F32),
            pltpu.VMEM((SPACE, 8, width), F32),
            pltpu.VMEM((STEPS, 3, 2, 8, HALF), F32),
            pltpu.VMEM((STEPS, GROUPS, SPACE, 16, HALF), BF16),
            pltpu.VMEM((GROUPS, 64, 2 * HALF), BF16),
            pltpu.VMEM((STEPS, GROUPS, 17, 2, 64, 256), BF16),
            pltpu.VMEM((GROUPS, 64, 256), F32),
            pltpu.VMEM((STEPS, GROUPS, 2, 32, 256), BF16),
            pltpu.VMEM((STEPS, GROUPS, 32, 256), BF16),
            pltpu.VMEM((STEPS, GROUPS, 4, 16, HALF), BF16),
            pltpu.VMEM((STEPS, GROUPS, 4, 16, HALF), BF16),
            pltpu.VMEM((STEPS, 24, 2 * HALF), F32),
            pltpu.VMEM((24, 2 * HALF), BF16),
            pltpu.VMEM((3, FREQ, width), BF16),
            dma((5,)),
            dma((2,)),
            dma((2, 8, 6)),
            dma((17,)),
            dma((2,)),
            dma((2,)),
            dma((2,)),
            dma,
            dma,
            dma((STEPS, GROUPS)),
            dma((STEPS, GROUPS)),
            dma((STEPS, GROUPS)),
            dma((STEPS, GROUPS)),
            dma((STEPS, GROUPS)),
            dma((STEPS, GROUPS)),
            dma((STEPS, GROUPS)),
            dma((STEPS, GROUPS)),
            dma((STEPS, GROUPS)),
            dma((STEPS, GROUPS, 9, 2)),
            dma((STEPS, GROUPS, 16)),
        ],
        compiler_params=pltpu.CompilerParams(
            collective_id=0, has_side_effects=True, vmem_limit_bytes=63 * 1024 * 1024
        ),
    )(
        hidden, qkv_weight, out_weight, jnp.transpose(mod_weight, (1, 0, 2)), omega[None],
        slot_frame, levels, timesteps,
    )


def solution(mesh):
    in_specs = (
        P("queue", "space", None),
        P(None, "queue", "space"),
        P("queue", "space"),
        P(None, None, "space"),
        P(),
        P(),
        P(),
    )
    out_specs = (P(None, "queue", "space", None), P("queue", "space", None))
    return jax.shard_map(shards, mesh=mesh, in_specs=in_specs, out_specs=out_specs, check_vma=False)
```

time: 155 us -> 135 us (0.87)
  Pallas kernels: 149 us -> 130 us
  local copies, waits for them, and re-layouts: 5.62 us -> 2.4 us
    pallas_call x1, Pallas kernels: 149 us -> 130 us  [shards(): pl.pallas_call(kernel, name='denoise', out_shape=(jax.ShapeDtypeStruct((S...]
    unnamed x16 -> x4, local copies, waits for them, and re-layouts: 5.62 us -> 2.4 us
where the time goes in v2:
time: 135 us; the launch traced here: 134 us
  Pallas kernels  130 us (96%)
  local copies, waits for them, and re-layouts  2.4 us (2%)
    pallas_call x1, Pallas kernels, shards(): pl.pallas_call(kernel, name='denoise', out_shape=(jax.ShapeDtypeStruct((S...  130 us

profile of v2, /device:TPU:1, one launch (start us, length us, event | category | flops | bytes accessed | tf_op | source)
XLA Modules:
  0.0 134.0 jit_solution(3894516021579938947)
XLA Ops:
  0.6 0.5 multiply_exponential_fusion.omega
  1.2 130.4 %denoise.1 = (bf16[2,1,24,3072]{3,2,1,0:T(8,128)(2,1)}, bf16[1,24,3072]{2,1,0:T(8,128)(2,1)}) custom-call(bf16[1,24,3072]{2,1,0:T(8,128)(2,1)} %hid.1, bf16[3,48,256]{2,1,0:T(8,128)(2,1)} %qkvw.1, bf16[48,256]{1,0:T(8,128)(2,1)} %outw.1, bf16[3,256,384]{2,1,0:T(8,128)(2,1)} %bitcast.1, f32[1,128]{1,0:T(1,128)} %multiply_exponential_fusion.omega, ...), custom_call_target="tpu_custom_call" | custom-call | tf_op jit(solution)/shard_map/denoise/pallas_call | solution.py:459
  131.6 0.0 copy-start
  131.6 1.7 %copy.11 = bf16[2,1,24,3072]{3,2,1,0:T(8,128)(2,1)} copy(bf16[2,1,24,3072]{3,2,1,0:T(8,128)(2,1)} %get-tuple-element.4) | data formatting | bytes 589824
  133.3 0.0 copy-done
  133.3 0.7 copy.12
Async XLA Ops:
  131.6 1.7 %copy-start = (bf16[1,24,3072]{2,1,0:T(8,128)(2,1)S(1)}, bf16[1,24,3072]{2,1,0:T(8,128)(2,1)}, u32[]{:S(2)}) copy-start(bf16[1,24,3072]{2,1,0:T(8,128)(2,1)} %get-tuple-element.5) | copy-start | bytes 442372

commit v3 on v2

--- a/solution.py
+++ b/solution.py
@@ -3,6 +3,7 @@
 
 import jax
 import jax.numpy as jnp
+import numpy as np
 from jax import lax
 from jax.experimental import pallas as pl
 from jax.experimental.pallas import tpu as pltpu
@@ -17,13 +18,20 @@
 GROUPS = 3
 HALF = 1536
 SPACE = 8
+ORDER = [("near", 0), ("near", 1), ("near", 2), (4, 0), (4, 1), (4, 2), ("share", 0), ("far", 0), ("far", 1),
+         ("shared", 0), ("far", 2), ("out", 0), ("out", 1), ("out", 2)]
+X_TURNS = {h: [] for h in range(1, 10)}
+for _j in range(16):
+    X_TURNS[(max(1, _j if _j <= 8 else _j - 8) + 1) if _j else 1].append(_j)
 FRAMES = 64
+FAR = (0, 1, 15)
+NEAR = tuple(w for w in range(16) if w not in FAR)
 
 
 def kernel(
     hid, qkvw, outw, modw, omega, slot_frame, levels, timesteps,
     vel_out, lat_out,
-    W, WX, XS, MP, MG, MODF, G, LHS, KV, QS, ATT, ATX, PB, RB, VO, HS, MW, in_sem,
+    W, WX, XS, MP, MG, MODF, G, LHS, KV, QS, NUM, DEN, ATT, ATX, PB, RB, VO, HS, MW, OM, in_sem,
     w_send, z_recv, x_recv, sib_recv, wx_send, wx_recv, mod_send, mod_recv,
     ag_send, ag_recv, agx_recv, agy_recv, at_send, at_recv, rs_send, rs_recv,
     kv_send, kv_recv, kvs_recv,
@@ -74,6 +82,7 @@
         pltpu.make_async_copy(outw, W.at[q // 2, c, 3], in_sem.at[2]),
         pltpu.make_async_copy(modw, MW, in_sem.at[3]),
         pltpu.make_async_copy(hid.at[0], HS, in_sem.at[4]),
+        pltpu.make_async_copy(omega, OM, in_sem.at[5]),
     ]
     for load in loads:
         load.start()
@@ -113,7 +122,8 @@
     dsigma = [(t_b - t_a) * (1.0 / 1000.0), (t_c - t_b) * (1.0 / 1000.0)]
 
     row = lax.broadcasted_iota(jnp.int32, (16, FREQ // 2), 0)
-    angle = jnp.where(row % 2 == 0, t_a, t_b) * omega[...]
+    loads[5].wait()
+    angle = jnp.where(row % 2 == 0, t_a, t_b) * OM[...]
     emb = jnp.concatenate([jnp.cos(angle), jnp.sin(angle)], axis=-1).astype(BF16)
     cols = SPACE * 48
     loads[3].wait()
@@ -308,29 +318,42 @@
         f = frame + (w - 8)
         masks.append(jnp.where((f >= 0) & (f < FRAMES), 1.0, 0.0).astype(F32))
 
-    def attend(st, g):
-        for w in range(1, 16, 2):
-            wait(KV.at[st, g, w], kvs_recv.at[st, g, w])
+    def attend(st, g, places, first, last):
+        for w in places:
+            if w % 2 == 1:
+                wait(KV.at[st, g, w], kvs_recv.at[st, g, w])
 
         def rows16(i, carry):
             at = pl.ds(pl.multiple_of(i * 16, 16), 16)
             for h in range(2):
                 lanes = pl.ds(h * HEAD_DIM, HEAD_DIM)
                 query = QS[g, at, lanes]
-                num = jnp.zeros((16, HEAD_DIM), F32)
-                den = jnp.zeros((16, 1), F32)
-                for w in range(16):
+                if first:
+                    num = jnp.zeros((16, HEAD_DIM), F32)
+                    den = jnp.zeros((16, HEAD_DIM), F32)
+                else:
+                    num, den = NUM[g, at, lanes], DEN[g, at, lanes]
+                for w in places:
                     key = KV[st, g, w, 0, at, lanes].astype(F32)
                     score = jnp.sum(query * key, axis=-1, keepdims=True)
                     e = jnp.exp(score) * masks[w]
                     den = den + e
                     num = num + e * KV[st, g, w, 1, at, lanes].astype(F32)
-                ATT[st, g, i // 2, pl.ds(pl.multiple_of((i % 2) * 16, 16), 16), lanes] = (
-                    num / den
-                ).astype(BF16)
+                if last:
+                    ATT[st, g, i // 2, pl.ds(pl.multiple_of((i % 2) * 16, 16), 16), lanes] = (
+                        num / den
+                    ).astype(BF16)
+                else:
+                    NUM[g, at, lanes], DEN[g, at, lanes] = num, den
             return carry
 
         lax.fori_loop(0, 4, rows16, 0)
+
+    def attend_near(st, g):
+        attend(st, g, NEAR, True, False)
+
+    def attend_far(st, g):
+        attend(st, g, FAR, False, True)
         send(ATT.at[st, g, 1 - xh], ATX.at[st, g], at_send.at[st, g], at_recv.at[st, g], hdev)
 
     def out_send(st, g):
@@ -367,60 +390,63 @@
             VO[st, 8 * g : 8 * g + 8, half * HALF : (half + 1) * HALF] = vel
             XS[g, half] = (cur + dsigma[st] * vel).astype(BF16).astype(F32)
 
+    def queries_outputs(h):
+        if h <= 8:
+            for m in (4, 5):
+                relay(h, 0, m)
+                relay(h, 1, m)
+        for j in X_TURNS[h]:
+            take_x(j)
+
     for h in range(1, 9):
-        for m in range(6):
+        for m in range(4):
             relay(h, 0, m)
             relay(h, 1, m)
             if h == 1 and m == 1:
                 seed()
+        queries_outputs(h)
         if h == 1:
-            take_x(0)
             spread_modulation()
-        else:
-            take_x(h - 1)
-            take_x(8 + h - 1)
         if 2 <= h <= 4:
             norm_send(0, h - 2)
         if 5 <= h <= 7:
             norm_pass(0, h - 5)
-    take_x(8)
+    queries_outputs(9)
     partner_weights()
     wait(W.at[pl.ds(0, 16), pl.ds(0, 2), kv_half], sib_recv.at[0])
 
+    def start(st, g):
+        take_rows(st, g)
+        project_kv(st, g)
+
+    order = (
+        [("start", g) for g in range(3)] + [("weights", 0)] + [("query", g) for g in range(3)]
+        + [(h, g) for h in range(1, 4) for g in range(3)] + [("velocity", 0)]
+        + ORDER
+    )
+    calls = {
+        "start": start, "near": attend_near, "far": attend_far, "out": out_send,
+        "query": lambda st, g: project_q(st, g),
+        "weights": lambda st, g: st == 0 and finish_weights(),
+        "share": lambda st, g: st == 0 and share_partner_weights(),
+        "shared": lambda st, g: st == 0 and finish_partner_weights(),
+    }
     for st in range(STEPS):
-        for g in range(GROUPS):
-            take_rows(st, g)
-            project_kv(st, g)
-        if st == 0:
-            finish_weights()
-        for g in range(GROUPS):
-            project_q(st, g)
-        for h in range(1, 4):
-            for g in range(GROUPS):
-                kv_relay(st, g, h)
-        if st == 0:
-            share_partner_weights()
-        else:
-            vel_out[0, 0] = VO[0].astype(BF16)
-        kv_relay(st, 0, 4)
-        kv_relay(st, 1, 4)
-        attend(st, 0)
-        kv_relay(st, 2, 4)
-        attend(st, 1)
-        if st == 0:
-            finish_partner_weights()
-        out_send(st, 0)
-        attend(st, 2)
-        out_send(st, 1)
-        out_send(st, 2)
+        for what, g in order:
+            if what == "velocity":
+                if st == 1:
+                    vel_out[0, 0] = VO[0].astype(BF16)
+            elif what in calls:
+                calls[what](st, g)
+            else:
+                kv_relay(st, g, what)
         for g in range(GROUPS):
             update(st, g)
             if st + 1 < STEPS:
                 norm_send(st + 1, g)
-                if g > 0:
-                    norm_pass(st + 1, g - 1)
         if st + 1 < STEPS:
-            norm_pass(st + 1, GROUPS - 1)
+            for g in range(GROUPS):
+                norm_pass(st + 1, g)
 
     vel_out[1, 0] = VO[1].astype(BF16)
     for g in range(GROUPS):
@@ -450,7 +476,7 @@
 
 def shards(hidden, qkv_weight, out_weight, mod_weight, slot_frame, levels, timesteps):
     half_freq = FREQ // 2
-    omega = jnp.exp(-math.log(10000.0) * jnp.arange(half_freq).astype(F32) / half_freq)
+    omega = np.exp(-math.log(10000.0) * np.arange(half_freq) / half_freq).astype(np.float32)
     vmem = pl.BlockSpec(memory_space=pltpu.VMEM)
     hbm = pl.BlockSpec(memory_space=pltpu.HBM)
     smem = pl.BlockSpec(memory_space=pltpu.SMEM)
@@ -463,7 +489,7 @@
             jax.ShapeDtypeStruct((STEPS, 1, 24, 2 * HALF), BF16),
             jax.ShapeDtypeStruct((1, 24, 2 * HALF), BF16),
         ),
-        in_specs=[hbm] * 4 + [vmem] + [smem] * 3,
+        in_specs=[hbm] * 5 + [smem] * 3,
         out_specs=(vmem, vmem),
         scratch_shapes=[
             pltpu.VMEM((FRAMES // 2, 2, 4, 48, 256), BF16),
@@ -476,6 +502,8 @@
             pltpu.VMEM((GROUPS, 64, 2 * HALF), BF16),
             pltpu.VMEM((STEPS, GROUPS, 17, 2, 64, 256), BF16),
             pltpu.VMEM((GROUPS, 64, 256), F32),
+            pltpu.VMEM((GROUPS, 64, 256), F32),
+            pltpu.VMEM((GROUPS, 64, 256), F32),
             pltpu.VMEM((STEPS, GROUPS, 2, 32, 256), BF16),
             pltpu.VMEM((STEPS, GROUPS, 32, 256), BF16),
             pltpu.VMEM((STEPS, GROUPS, 4, 16, HALF), BF16),
@@ -483,7 +511,8 @@
             pltpu.VMEM((STEPS, 24, 2 * HALF), F32),
             pltpu.VMEM((24, 2 * HALF), BF16),
             pltpu.VMEM((3, FREQ, width), BF16),
-            dma((5,)),
+            pltpu.VMEM((1, FREQ // 2), F32),
+            dma((6,)),
             dma((2,)),
             dma((2, 8, 6)),
             dma((17,)),

time: 135 us -> 133 us (0.985)
    pallas_call x1, Pallas kernels: 130 us -> 129 us  [shards(): pl.pallas_call(kernel, name='denoise', out_shape=(jax.ShapeDtypeStruct((S...]
where the time goes in v3:
time: 133 us; the launch traced here: 132 us
  Pallas kernels  129 us (97%)
  local copies, waits for them, and re-layouts  2.4 us (2%)
    pallas_call x1, Pallas kernels, shards(): pl.pallas_call(kernel, name='denoise', out_shape=(jax.ShapeDtypeStruct((S...  129 us

profile of v3, /device:TPU:1, one launch (start us, length us, event | category | flops | bytes accessed | tf_op | source)
XLA Modules:
  0.0 132.1 jit_solution(13029428127966553401)
XLA Ops:
  0.6 129.0 %denoise.1 = (bf16[2,1,24,3072]{3,2,1,0:T(8,128)(2,1)}, bf16[1,24,3072]{2,1,0:T(8,128)(2,1)}) custom-call(bf16[1,24,3072]{2,1,0:T(8,128)(2,1)} %hid.1, bf16[3,48,256]{2,1,0:T(8,128)(2,1)} %qkvw.1, bf16[48,256]{1,0:T(8,128)(2,1)} %outw.1, bf16[3,256,384]{2,1,0:T(8,128)(2,1)} %bitcast.1, f32[1,128]{1,0:T(1,128)} %constant.2.clone.omega, s32[64]{0:T(128)} %slot_frame.1, ...), custom_call_target="tpu_custom_call" | custom-call | tf_op jit(solution)/shard_map/denoise/pallas_call | solution.py:485
  129.7 0.0 copy-start
  129.7 1.7 %copy.12 = bf16[2,1,24,3072]{3,2,1,0:T(8,128)(2,1)} copy(bf16[2,1,24,3072]{3,2,1,0:T(8,128)(2,1)} %get-tuple-element.4) | data formatting | bytes 589824
  131.4 0.0 copy-done
  131.4 0.7 copy.13
Async XLA Ops:
  129.7 1.7 %copy-start = (bf16[1,24,3072]{2,1,0:T(8,128)(2,1)S(1)}, bf16[1,24,3072]{2,1,0:T(8,128)(2,1)}, u32[]{:S(2)}) copy-start(bf16[1,24,3072]{2,1,0:T(8,128)(2,1)} %get-tuple-element.5) | copy-start | bytes 442372

commit v4 on v3

--- a/solution.py
+++ b/solution.py
@@ -217,9 +217,9 @@
         right = right * inv * MODF[st, 1, 1] + MODF[st, 0, 1]
         G[st, g, slot] = jnp.concatenate([left, right], axis=0).astype(BF16)
         g_move(st, g, slot, agx_recv.at[st, g], hdev)
+        g_move(st, g, slot, agy_recv.at[st, g], ydevs[2])
         g_move(st, g, slot, ag_recv.at[st, g], ydevs[0])
         g_move(st, g, slot, ag_recv.at[st, g], ydevs[1])
-        g_move(st, g, slot, agy_recv.at[st, g], ydevs[2])
 
     def norm_pass(st, g):
         other = (1 - xh) * 4 + y
@@ -375,7 +375,7 @@
                 pair.append(total.reshape(4, 8, 768))
             PB[st, g, :, :, 768 * j : 768 * (j + 1)] = jnp.concatenate(pair, axis=1).astype(BF16)
         RB[st, g, y] = PB[st, g, y]
-        for k, dev in zip((1, 3, 2), ydevs):
+        for k, dev in zip((2, 1, 3), (ydevs[2], ydevs[0], ydevs[1])):
             send(
                 PB.at[st, g, (y + k) % 4], RB.at[st, g, y],
                 rs_send.at[st, g], rs_recv.at[st, g], dev,

time: 133 us -> 133 us (level)
  no operation moved by 1% of the time
where the time goes in v4:
time: 133 us; the launch traced here: 132 us
  Pallas kernels  129 us (97%)
  local copies, waits for them, and re-layouts  2.4 us (2%)
    pallas_call x1, Pallas kernels, shards(): pl.pallas_call(kernel, name='denoise', out_shape=(jax.ShapeDtypeStruct((S...  129 us

profile of v4, /device:TPU:1, one launch (start us, length us, event | category | flops | bytes accessed | tf_op | source)
XLA Modules:
  0.0 132.5 jit_solution(3327245997323654187)
XLA Ops:
  0.6 129.4 %denoise.1 = (bf16[2,1,24,3072]{3,2,1,0:T(8,128)(2,1)}, bf16[1,24,3072]{2,1,0:T(8,128)(2,1)}) custom-call(bf16[1,24,3072]{2,1,0:T(8,128)(2,1)} %hid.1, bf16[3,48,256]{2,1,0:T(8,128)(2,1)} %qkvw.1, bf16[48,256]{1,0:T(8,128)(2,1)} %outw.1, bf16[3,256,384]{2,1,0:T(8,128)(2,1)} %bitcast.1, f32[1,128]{1,0:T(1,128)} %constant.2.clone.omega, s32[64]{0:T(128)} %slot_frame.1, ...), custom_call_target="tpu_custom_call" | custom-call | tf_op jit(solution)/shard_map/denoise/pallas_call | solution.py:485
  130.1 0.0 copy-start
  130.1 1.7 %copy.12 = bf16[2,1,24,3072]{3,2,1,0:T(8,128)(2,1)} copy(bf16[2,1,24,3072]{3,2,1,0:T(8,128)(2,1)} %get-tuple-element.4) | data formatting | bytes 589824
  131.8 0.0 copy-done
  131.8 0.7 copy.13
Async XLA Ops:
  130.1 1.7 %copy-start = (bf16[1,24,3072]{2,1,0:T(8,128)(2,1)S(1)}, bf16[1,24,3072]{2,1,0:T(8,128)(2,1)}, u32[]{:S(2)}) copy-start(bf16[1,24,3072]{2,1,0:T(8,128)(2,1)} %get-tuple-element.5) | copy-start | bytes 442372
